TPU v7x, 256 devices: a whole 4x4x8 slice. The times are simulated.
256 devices in a mesh: leaf: 4 (over x), row: 8 (over z), col: 8 (over y, core).
Axes of the slice: x: 4, y: 4, z: 8, core: 2. Of those that a mesh axis runs over, the one named last changes fastest.
Arguments:
- child_rhs: bfloat16 [4, 2, 8, 256, 256], P('leaf', None, 'col'), may hold values from -6 to 6
- child_inv: bfloat16 [4, 2, 8, 256, 2, 8, 256], P('leaf', None, 'row', None, None, 'col')
- root_inv: bfloat16 [6, 8, 256, 6, 8, 256], P(None, 'row', None, None, 'col')
- coupling: bfloat16 [4, 2, 8, 256, 3, 8, 256], P('leaf', None, 'row', None, None, 'col'), may hold values from -0.09375 to 0.09375
- root_rhs: bfloat16 [6, 8, 256, 256], P(None, 'col'), may hold values from -6 to 6
- structure: int32 [4, 24], P('leaf'), may hold values from 0 to 47, as said below
Outputs:
- child_solution: float32 [4, 2, 8, 256, 256], P('leaf', None, 'col')
- root_solution: float32 [6, 8, 256, 256], P(None, 'col')
Inputs may be any that keep to these rules, and one draw needn't show every extreme that they name: `structure`: within one child the 24 entries are distinct; different children may share root blocks.
All inputs are finite; a program needn't handle non-finite values.
Results may differ from a plain program's by a relative error of at most 0.008.
Values may be sent and summed in bfloat16 or wider, within the bound.
A program may use at most 64 MiB of HBM per device.

v0:
```python
import jax
import jax.numpy as jnp
from jax import lax
from jax.sharding import PartitionSpec as P


def on_device(child_rhs, child_inv, root_inv, coupling, root_rhs, structure):
    leaves = lax.axis_size("leaf")
    row_count = lax.axis_size("row")
    col_count = lax.axis_size("col")
    col_place = lax.axis_index("col")
    block_size = child_inv.shape[3]
    rhs_cols = child_rhs.shape[4]
    child_m = child_inv[0, :, 0, :, :, 0, :]
    child_b = child_rhs[0, :, 0]
    root_m = root_inv[:, 0, :, :, 0, :]
    link_m = coupling[0, :, 0, :, :, 0, :]
    root_b = root_rhs[:, 0]
    link_count = link_m.shape[2]
    root_cols = root_m.shape[2]
    link_ids = structure[0].reshape(link_count, col_count)
    col_pick = (jnp.arange(col_count) == col_place).astype(jnp.int32)
    my_links = jnp.sum(link_ids * col_pick[None, :], axis=1)
    partial_value = jnp.einsum(
        "abxc,xcn->abn", child_m, child_b, preferred_element_type=jnp.float32
    )
    forward = lax.psum(partial_value, "col")
    lifted = jnp.einsum(
        "abmc,abn->mcn", link_m, forward.astype(jnp.bfloat16), preferred_element_type=jnp.float32
    )
    targets = jnp.arange(col_count)[:, None] + jnp.arange(root_cols)[None, :] * col_count
    slab_rows = root_cols * block_size // (leaves * row_count)
    dense_term = jnp.zeros((col_count, root_cols, block_size, rhs_cols), jnp.float32)
    for link in range(link_count):
        hit = my_links[link] == targets
        dense_term = dense_term + jnp.where(hit[:, :, None, None], lifted[link][None, None], 0.0)
    dense_term = dense_term.reshape(col_count, leaves * row_count, slab_rows, rhs_cols)
    dense_term = dense_term.transpose(1, 0, 2, 3).reshape(-1, rhs_cols)
    my_piece = lax.psum_scatter(dense_term, ("leaf", "row", "col"), scatter_dimension=0, tiled=True)
    update = lax.all_gather(my_piece, ("leaf", "row"), axis=0, tiled=True).reshape(
        root_cols, block_size, rhs_cols
    )
    residual = (root_b.astype(jnp.float32) - update).astype(jnp.bfloat16)
    y_partial = jnp.einsum("abxc,xcn->abn", root_m, residual, preferred_element_type=jnp.float32)
    root_y = lax.psum(y_partial, "col").astype(jnp.bfloat16)
    x_partial = jnp.einsum("abxc,abn->xcn", root_m, root_y, preferred_element_type=jnp.float32)
    root_x = lax.psum(x_partial, "row")
    root_xb = root_x.astype(jnp.bfloat16)
    whole_root = lax.all_gather(root_xb[:, None], "col", axis=1, tiled=True).reshape(
        root_cols * col_count, block_size, rhs_cols
    )
    choose = (my_links[:, None] == jnp.arange(root_cols * col_count)[None, :]).astype(jnp.bfloat16)
    needed = jnp.einsum(
        "mr,rcn->mcn", choose, whole_root, preferred_element_type=jnp.float32
    ).astype(jnp.bfloat16)
    back_partial = jnp.einsum("abmc,mcn->abn", link_m, needed, preferred_element_type=jnp.float32)
    carried = lax.psum(back_partial, "col")
    adjusted = (forward - carried).astype(jnp.bfloat16)
    child_partial = jnp.einsum(
        "abxc,abn->xcn", child_m, adjusted, preferred_element_type=jnp.float32
    )
    child_x = lax.psum(child_partial, "row")
    return (child_x[None, :, None], root_x[:, None])


def solution(mesh):
    placed = (
        P("leaf", None, "col", None, None),
        P("leaf", None, "row", None, None, "col", None),
        P(None, "row", None, None, "col", None),
        P("leaf", None, "row", None, None, "col", None),
        P(None, "col", None, None),
        P("leaf", None),
    )
    return jax.shard_map(
        on_device,
        mesh=mesh,
        in_specs=placed,
        out_specs=(P("leaf", None, "col", None, None), P(None, "col", None, None)),
        check_vma=False,
    )
```

profile of v0, /device:TPU:1, one launch (start us, length us, event | category | flops | bytes accessed | tf_op | source)
XLA Modules:
  0.0 1003.3 jit_solution(10006390337514493363)
XLA Ops:
  7.2 2.3 convolution_bitcast_fusion.3
  9.5 0.0 reduce-scatter.2.cloned.1.call-start
  9.6 0.5 broadcast.97
  10.1 1.3 reduce.3
  11.4 0.1 reshape_squeeze.3
  11.5 0.1 multiply_reduce_fusion
  11.6 0.7 fusion.37
  12.3 1.9 fusion.33
  14.2 0.1 broadcast_in_dim.107
  14.3 0.1 broadcast_in_dim.108
  14.4 0.1 broadcast_in_dim.110
  14.6 0.1 broadcast_in_dim.128
  14.6 0.1 broadcast_in_dim.129
  14.8 0.1 broadcast_in_dim.131
  14.9 0.1 broadcast_in_dim.118
  15.0 0.1 broadcast_in_dim.119
  15.2 0.1 broadcast_in_dim.121
  15.3 63.3 %all-reduce.6.cloned.1.call-done = f32[2,256,256]{2,1,0:T(8,128)} async-done(((f32[2,256,256]{2,1,0:T(8,128)}), f32[2,256,256]{2,1,0:T(8,128)}) %all-reduce.6.cloned.1.call-update) | async-done | bytes 524304 | tf_op jit(solution)/shard_map/psum | solution.py:27
  78.7 1.4 convolution_bitcast_fusion
  80.1 0.1 slice_bitcast_fusion.2
  80.2 0.1 copy.23
  80.3 0.1 copy.27
  80.4 0.1 copy.25
  80.6 0.1 broadcast_in_dim.124
  80.7 0.1 broadcast_in_dim.134
  80.8 0.1 broadcast_in_dim.113
  81.0 87.3 %fusion = f32[12288,256]{1,0:T(8,128)} fusion(f32[32,48,256]{2,1,0:T(8,128)S(1)} %bitcast.117, f32[32,48,256]{2,1,0:T(8,128)S(1)} %bitcast.116, f32[32,48,256]{2,1,0:T(8,128)S(1)} %bitcast.118, pred[12288]{0:T(1024)(128)(4,1)S(1)} %broadcast_in_dim.131, pred[12288]{0:T(1024)(128)(4,1)S(1)} %broadcast_in_dim.121, pred[12288]{0:T(1024)(128)(4,1)S(1)} %broadcast_in_dim.110), kind=kLoop, calls=%fused_computation.1 | loop fusion | flops 15728640 | bytes 17338368 | tf_op jit(solution)/shard_map/add | solution.py:36
  168.3 0.0 all-gather.4.cloned.1.call-start
  168.3 403.3 %reduce-scatter.2.cloned.1.call-done = f32[48,256]{1,0:T(8,128)} async-done(((f32[12288,256]{1,0:T(8,128)}), f32[48,256]{1,0:T(8,128)}) %reduce-scatter.2.cloned.1.call-update) | async-done | bytes 49168 | tf_op jit(solution)/shard_map/reduce_scatter | solution.py:39
  571.7 0.0 all-reduce.8.cloned.1.call-start
  571.7 78.2 %all-gather.4.cloned.1.call-done = f32[1536,256]{1,0:T(8,128)} async-done(((f32[48,256]{1,0:T(8,128)}), f32[1536,256]{1,0:T(8,128)}) %all-gather.4.cloned.1.call-update) | async-done | bytes 1572880 | tf_op jit(solution)/shard_map/all_gather | solution.py:40
  649.9 4.3 fusion.9
  654.2 54.8 %all-reduce.13 = bf16[6,256,256]{1,2,0:T(8,128)(2,1)S(1)} all-reduce(f32[6,256,256]{1,2,0:T(8,128)S(1)} %fusion.9), channel_id=1, replica_groups=mesh['leaf'=4,'row'=8,'col'=8] {'col'}, use_global_device_ids=true, to_apply=%region_3.4 | all-reduce | flops 393216 | bytes 2359296 | tf_op jit(solution)/shard_map/psum | solution.py:45
  709.1 4.9 fusion.12
  714.0 0.0 all-gather.6.cloned.1.call-start
  714.0 73.2 %all-reduce.8.cloned.1.call-done = f32[6,256,256]{1,2,0:T(8,128)} async-done(((f32[6,256,256]{1,2,0:T(8,128)}), f32[6,256,256]{1,2,0:T(8,128)}) %all-reduce.8.cloned.1.call-update) | async-done | bytes 1572880 | tf_op jit(solution)/shard_map/psum | solution.py:47
  787.2 2.4 convert_element_type.38
  789.6 0.0 all-reduce.10.cloned.1.call-start
  789.7 50.9 %all-gather.6.cloned.1.call-done = bf16[6,2048,256]{1,2,0:T(8,128)(2,1)} async-done(((bf16[6,256,256]{1,2,0:T(8,128)(2,1)}), bf16[6,2048,256]{1,2,0:T(8,128)(2,1)}) %all-gather.6.cloned.1.call-update) | async-done | bytes 6291472 | tf_op jit(solution)/shard_map/all_gather | solution.py:49
  840.6 8.6 copy.29
  849.2 6.5 fusion.2
  855.7 1.2 convolution_bitcast_fusion.2
  856.9 0.0 all-reduce.12.cloned.1.call-start
  856.9 64.5 %all-reduce.10.cloned.1.call-done = f32[2,256,256]{2,1,0:T(8,128)} async-done(((f32[2,256,256]{2,1,0:T(8,128)}), f32[2,256,256]{2,1,0:T(8,128)}) %all-reduce.10.cloned.1.call-update) | async-done | bytes 524304 | tf_op jit(solution)/shard_map/psum | solution.py:57
  921.4 2.2 convolution_bitcast_fusion.1
  923.6 1.6 copy.33
  925.3 69.2 %all-reduce.12.cloned.1.call-done = f32[1,2,1,256,256]{3,4,1,2,0:T(8,128)} async-done(((f32[1,2,1,256,256]{3,4,1,2,0:T(8,128)}), f32[1,2,1,256,256]{3,4,1,2,0:T(8,128)}) %all-reduce.12.cloned.1.call-update) | async-done | bytes 524304 | tf_op jit(solution)/shard_map/psum | solution.py:62
  994.4 2.0 copy.32
  (23 shorter events, 0.2 us)
Async XLA Ops:
  7.2 71.5 %copy-start = (bf16[1,2,1,256,3,1,256]{6,3,5,4,2,1,0:T(8,128)(2,1)S(1)}, bf16[1,2,1,256,3,1,256]{6,3,5,4,2,1,0:T(8,128)(2,1)}, u32[]{:S(2)}) copy-start(bf16[1,2,1,256,3,1,256]{6,3,5,4,2,1,0:T(8,128)(2,1)} %param.9) | copy-start | bytes 2359300
  7.2 71.5 %all-reduce.6.cloned.1.call-start = ((), (), s32[]{:S(2)}) async-start(), calls=%async_computation.1 | async-start | bytes 1048576 | tf_op jit(solution)/shard_map/psum | solution.py:27
  9.5 562.1 %reduce-scatter.2.cloned.1.call-start = ((), (), s32[]{:S(2)}) async-start(), calls=%async_computation.2 | async-start | bytes 12632064 | tf_op jit(solution)/shard_map/reduce_scatter | solution.py:39
  168.3 481.7 %copy-start.4 = (bf16[6,1,256,256]{3,2,1,0:T(8,128)(2,1)S(1)}, bf16[6,1,256,256]{3,2,1,0:T(8,128)(2,1)}, u32[]{:S(2)}) copy-start(bf16[6,1,256,256]{3,2,1,0:T(8,128)(2,1)} %param.10) | copy-start | bytes 2359300
  168.3 481.7 %all-gather.4.cloned.1.call-start = ((), (), s32[]{:S(2)}) async-start(), calls=%async_computation.3 | async-start | bytes 1622016 | tf_op jit(solution)/shard_map/all_gather | solution.py:40
  571.7 215.6 %all-reduce.8.cloned.1.call-start = ((), (), s32[]{:S(2)}) async-start(), calls=%async_computation.4 | async-start | bytes 3145728 | tf_op jit(solution)/shard_map/psum | solution.py:47
  714.0 126.6 %all-gather.6.cloned.1.call-start = ((), (), s32[]{:S(2)}) async-start(), calls=%async_computation.7 | async-start | bytes 7077888 | tf_op jit(solution)/shard_map/all_gather | solution.py:49
  789.6 131.8 %all-reduce.10.cloned.1.call-start = ((), (), s32[]{:S(2)}) async-start(), calls=%async_computation.5 | async-start | bytes 1048576 | tf_op jit(solution)/shard_map/psum | solution.py:57
  849.2 72.2 %copy-start.2 = (bf16[1,2,1,256,2,1,256]{6,4,5,3,2,1,0:T(2,128)(2,1)S(1)}, bf16[1,2,1,256,2,1,256]{6,4,5,3,2,1,0:T(2,128)(2,1)}, u32[]{:S(2)}) copy-start(bf16[1,2,1,256,2,1,256]{6,4,5,3,2,1,0:T(2,128)(2,1)} %param.7) | copy-start | bytes 1572868
  849.2 72.2 %copy-start.3 = (f32[2,256,256]{2,1,0:T(8,128)S(1)}, f32[2,256,256]{2,1,0:T(8,128)}, u32[]{:S(2)}) copy-start(f32[2,256,256]{2,1,0:T(8,128)} %all-reduce.6.cloned.1.call-done) | copy-start | bytes 1572868
  849.2 74.4 %copy-start.1 = (f32[6,256,256]{1,2,0:T(8,128)S(1)}, f32[6,256,256]{1,2,0:T(8,128)}, u32[]{:S(2)}) copy-start(f32[6,256,256]{1,2,0:T(8,128)} %all-reduce.8.cloned.1.call-done) | copy-start | bytes 4718596
  856.9 137.5 %all-reduce.12.cloned.1.call-start = ((), (), s32[]{:S(2)}) async-start(), calls=%async_computation.6 | async-start | bytes 1048576 | tf_op jit(solution)/shard_map/psum | solution.py:62
Sparse Core Ops, SparseCore 0:
  10.9 67.6 all-reduce.5
  168.4 403.1 reduce-scatter.1
  574.6 75.3 all-gather.3
  714.1 73.0 all-reduce.7
  789.7 50.8 all-gather.5
  857.0 64.3 all-reduce.9
  924.3 70.0 all-reduce.11
where the time goes:
time: 1010 us; the launch traced here: 1000 us
  waiting for transfers between devices  803 us (80%)
  other arithmetic  93 us (9%)
  blocking collectives  54.8 us (5%)
  matrix products  22.6 us (2%)
  local copies, waits for them, and re-layouts  15.5 us (2%)
  between operations  14.3 us (1%)
    reduce_scatter x1, waiting for transfers between devices, on_device(): lax.psum_scatter(dense_term, ('leaf', 'row', 'col'), scatter_dimension=0,...  403 us
    add x1, other arithmetic, on_device(): dense_term + jnp.where(hit[:, :, None, None], lifted[link][None, None], 0.0)  87.3 us
    all_gather x1, waiting for transfers between devices, on_device(): lax.all_gather(my_piece, ('leaf', 'row'), axis=0, tiled=True)  78.2 us
    psum x1, waiting for transfers between devices, on_device(): root_x = lax.psum(x_partial, 'row')  73.2 us
    psum x1, waiting for transfers between devices, on_device(): child_x = lax.psum(child_partial, 'row')  69.2 us
    psum x1, waiting for transfers between devices, on_device(): carried = lax.psum(back_partial, 'col')  64.5 us
    psum x1, waiting for transfers between devices, on_device(): forward = lax.psum(partial_value, 'col')  63.3 us
    psum x1, blocking collectives, on_device(): root_y = lax.psum(y_partial, 'col').astype(jnp.bfloat16)  54.8 us
  transfers between devices with their start and end apart: 7, of which 7 were waited for; matrix products, arithmetic and copies ran while one was open for 1% of the time, Pallas kernels for 0%

commit v1 on v0

v1 whole, which is shorter than its diff:
```python
import jax
import jax.numpy as jnp
from jax import lax
from jax.experimental import pallas as pl
from jax.experimental.pallas import tpu as pltpu
from jax.sharding import PartitionSpec as P

F32 = jnp.float32
BF16 = jnp.bfloat16
MESH = pl.DeviceIdType.MESH

(F_RS, F_AG, L_RS, L_X, L_C, U_AG, Y_RS, Y_AG, X_RS, X_C, N_X, N_AG, C_RS, A_AG, D_RS, D_AG,
 S_X, O_AG, O_X) = range(19)
TRANSFERS = 19


def swap_halves(v):
    flat = v.reshape(-1, 128)
    return pltpu.roll(flat, 64, 1).reshape(v.shape)


def left_half(shape):
    return lax.broadcasted_iota(jnp.int32, shape, len(shape) - 1) < 64


def pack_quarters(top, bottom):
    left = left_half(top.shape)
    return jnp.where(left, top, swap_halves(bottom)), jnp.where(left, swap_halves(top), bottom)


def kernel(
    child_h, rhs_h, link_h, root_h, root_rhs_h, structure_ref,
    child_out, root_out,
    child, rhs, link, root, root_rhs, child_t, link_t, root_t,
    f_send, f_recv, f_mine, f_all, l_send, l_recv, lx_send, lx_all, c_send, c_recv,
    u_all, spread, y_send, y_recv, y_all, x_send, x_recv, x_all, n_send, n_recv, n_all,
    c2_send, c2_recv, a_all, d_send, d_recv, d_all, o_all, o_recv,
    ids_v, ids, local_sem, send_sem, recv_sem,
):
    leaf, row, col = (lax.axis_index(a) for a in ("leaf", "row", "col"))
    place = {"leaf": leaf, "row": row, "col": col}
    size = {"leaf": 4, "row": 8, "col": 8}
    started = []

    def peer(axis, step):
        return lax.rem(place[axis] + step, size[axis])

    def start(number, axis, source, target):
        copies = []
        for step in range(1, size[axis]):
            there = peer(axis, step)
            copy = pltpu.make_async_remote_copy(
                src_ref=source(there), dst_ref=target(step),
                send_sem=send_sem.at[number, step], recv_sem=recv_sem.at[number, step],
                device_id={axis: there}, device_id_type=MESH,
            )
            copy.start()
            copies.append(copy)
        started.extend(copies)
        return copies

    def scatter(number, axis, parts, landing):
        return start(number, axis, lambda there: parts.at[there], lambda step: landing.at[step])

    def gather(number, axis, whole):
        mine = whole.at[place[axis]]
        return start(number, axis, lambda there: mine, lambda step: mine)

    def arrived(copies):
        for copy in copies:
            copy.wait_recv()

    def total(axis, parts, landing):
        value = parts[place[axis]].astype(F32)
        for step in range(1, size[axis]):
            value = value + landing[step].astype(F32)
        return value

    def dot(a, b):
        return jnp.dot(a, b, preferred_element_type=F32)

    loads = [
        pltpu.make_async_copy(src, dst, local_sem.at[n])
        for n, (src, dst) in enumerate(
            ((child_h, child), (rhs_h, rhs), (link_h, link), (root_rhs_h, root_rhs), (root_h, root))
        )
    ]
    for load in loads:
        load.start()

    barrier = pltpu.get_barrier_semaphore()
    for axis in ("leaf", "row", "col"):
        for step in range(1, size[axis]):
            pl.semaphore_signal(barrier, inc=1, device_id={axis: peer(axis, step)}, device_id_type=MESH)
    pl.semaphore_wait(barrier, 17)

    structure_copies = start(
        S_X, "leaf", lambda there: structure_ref, lambda step: ids_v.at[leaf]
    )
    ids_v[leaf] = structure_ref[...]

    loads[0].wait()
    loads[1].wait()
    for a in range(2):
        part = dot(child[a, 0], rhs[0]) + dot(child[a, 1], rhs[1])
        f_send[pl.ds(4 * a, 4)] = part.reshape(4, 64, 256).astype(BF16)
    copies = scatter(F_RS, "col", f_send, f_recv)
    loads[2].wait()
    for a in range(2):
        for m in range(3):
            link_t[m, a] = link[a, m].T
    arrived(copies)
    f_mine[...] = total("col", f_send, f_recv)
    f_all[col] = f_mine[...].astype(BF16)
    copies = gather(F_AG, "col", f_all)
    for a in range(2):
        for x in range(2):
            child_t[x, a] = child[a, x].T
    loads[3].wait()
    loads[4].wait()
    arrived(copies)

    for m in range(3):
        part = jnp.zeros((256, 256), F32)
        for a in range(2):
            part = part + dot(link_t[m, a], f_all[pl.ds(4 * a, 4)].reshape(256, 256))
        l_send[:, m] = part.reshape(8, 32, 256).astype(BF16)
    copies = scatter(L_RS, "row", l_send, l_recv)

    def turn(n, carry):
        a, x = n // 6, n % 6
        root_t[x * 6 + a] = root[a * 6 + x].T
        return carry

    lax.fori_loop(0, 36, turn, 0)
    arrived(structure_copies)
    to_scalars = pltpu.make_async_copy(ids_v, ids, local_sem.at[5])
    to_scalars.start()
    to_scalars.wait()
    arrived(copies)
    lifted = total("row", l_send, l_recv)
    for h in range(2):
        lanes = lifted[:, :, 128 * h : 128 * h + 128]
        for q, packed in enumerate(pack_quarters(lanes[:, :16], lanes[:, 16:])):
            lx_send[2 * h + q] = packed.astype(BF16)
    copies = start(L_X, "leaf", lambda there: lx_send.at[there], lambda step: lx_all.at[leaf])
    lx_all[leaf] = lx_send[leaf]
    arrived(copies)

    block = lax.broadcasted_iota(jnp.int32, (6, 16, 128), 0) * 8
    for target in range(8):
        value = jnp.zeros((6, 16, 128), F32)
        for child_at in range(4):
            for m in range(3):
                wanted = ids[child_at, 0, col + 8 * m] - target
                value = value + jnp.where(block == wanted, lx_all[child_at, m].astype(F32)[None], 0.0)
        c_send[target] = value.astype(BF16)
    copies = scatter(L_C, "col", c_send, c_recv)
    base = root_rhs[:, pl.ds(pl.multiple_of(row * 32, 32), 32), pl.ds(pl.multiple_of((leaf // 2) * 128, 128), 128)]
    base = base.astype(F32)
    first, second = pack_quarters(base[:, :16], base[:, 16:])
    base = jnp.where(leaf % 2 == 0, first, second)
    arrived(copies)
    update = total("col", c_send, c_recv)
    u_all[row] = (base - update).astype(BF16)
    copies = gather(U_AG, "row", u_all)
    left = left_half((8, 16, 128))
    keep_left = jnp.where(left, 1.0, 0.0).astype(BF16)
    keep_right = jnp.where(left, 0.0, 1.0).astype(BF16)

    def spread_out(whole):
        for a in range(6):
            spread[a, :, 0] = whole[:, a] * keep_left
            spread[a, :, 1] = whole[:, a] * keep_right

    def root_product(matrix, parts):
        for a in range(6):
            value = jnp.zeros((256, 128), F32)
            for x in range(6):
                value = value + dot(matrix[a * 6 + x], spread[x].reshape(256, 128))
            value = value + swap_halves(value)
            value = value.reshape(8, 2, 16, 128)
            parts[:, a] = jnp.where(left, value[:, 0], value[:, 1]).astype(BF16)

    arrived(copies)
    spread_out(u_all)
    root_product(root, y_send)
    copies = scatter(Y_RS, "col", y_send, y_recv)
    arrived(copies)
    y_all[col] = total("col", y_send, y_recv).astype(BF16)
    copies = gather(Y_AG, "col", y_all)
    arrived(copies)
    spread_out(y_all)
    root_product(root_t, x_send)
    copies = scatter(X_RS, "row", x_send, x_recv)
    arrived(copies)
    solved = total("row", x_send, x_recv).astype(BF16)
    x_all[col] = solved
    copies = gather(X_C, "col", x_all)
    o_all[row] = solved
    out_copies = gather(O_AG, "row", o_all)
    arrived(copies)

    for child_at in range(4):
        for m in range(3):
            r = ids[child_at, 0, col + 8 * m]
            n_send[child_at, m] = x_all[r & 7, r >> 3]
    copies = start(N_X, "leaf", lambda there: n_send.at[there], lambda step: n_recv.at[leaf])
    n_recv[leaf] = n_send[leaf]

    def unpack(even, odd):
        even, odd = even.astype(F32), odd.astype(F32)
        mask = left_half(even.shape)
        top = jnp.where(mask, even, swap_halves(odd))
        bottom = jnp.where(mask, swap_halves(even), odd)
        return top.astype(BF16), bottom.astype(BF16)

    arrived(copies)
    for h in range(2):
        top, bottom = unpack(n_recv[2 * h], n_recv[2 * h + 1])
        n_all[row, :, pl.ds(0, 16), pl.ds(128 * h, 128)] = top
        n_all[row, :, pl.ds(16, 16), pl.ds(128 * h, 128)] = bottom
    copies = gather(N_AG, "row", n_all)
    arrived(copies)

    for a in range(2):
        part = jnp.zeros((256, 256), F32)
        for m in range(3):
            part = part + dot(link[a, m], n_all[:, m].reshape(256, 256))
        c2_send[pl.ds(4 * a, 4)] = part.reshape(4, 64, 256).astype(BF16)
    copies = scatter(C_RS, "col", c2_send, c2_recv)
    arrived(out_copies)
    o_recv[leaf] = o_all[...]
    out_copies = start(O_X, "leaf", lambda there: o_all, lambda step: o_recv.at[leaf])
    arrived(copies)
    a_all[col] = (f_mine[...] - total("col", c2_send, c2_recv)).astype(BF16)
    copies = gather(A_AG, "col", a_all)
    arrived(copies)

    for x in range(2):
        part = jnp.zeros((256, 256), F32)
        for a in range(2):
            part = part + dot(child_t[x, a], a_all[pl.ds(4 * a, 4)].reshape(256, 256))
        d_send[pl.ds(4 * x, 4)] = part.reshape(4, 64, 256).astype(BF16)
    copies = scatter(D_RS, "row", d_send, d_recv)
    arrived(out_copies)
    for h in range(2):
        for r in range(8):
            top, bottom = unpack(o_recv[2 * h, r], o_recv[2 * h + 1, r])
            root_out[:, pl.ds(32 * r, 16), pl.ds(128 * h, 128)] = top
            root_out[:, pl.ds(32 * r + 16, 16), pl.ds(128 * h, 128)] = bottom
    arrived(copies)
    d_all[row] = total("row", d_send, d_recv).astype(BF16)
    copies = gather(D_AG, "row", d_all)
    arrived(copies)
    child_out[...] = d_all[...]
    for copy in started:
        copy.wait_send()


def on_device(child_rhs, child_inv, root_inv, coupling, root_rhs, structure):
    child = child_inv[0, :, 0, :, :, 0, :].transpose(0, 2, 1, 3)
    rhs = child_rhs[0, :, 0]
    link = coupling[0, :, 0, :, :, 0, :].transpose(0, 2, 1, 3)
    root = root_inv[:, 0, :, :, 0, :].transpose(0, 2, 1, 3).reshape(36, 256, 256)
    away = pl.BlockSpec(memory_space=pl.ANY)
    near = pl.BlockSpec(memory_space=pltpu.VMEM)
    packed = (6, 16, 128)
    shapes = [
        (2, 2, 256, 256), (2, 256, 256), (2, 3, 256, 256), (36, 256, 256), (6, 256, 256),
        (2, 2, 256, 256), (3, 2, 256, 256), (36, 256, 256),
        (8, 64, 256), (8, 64, 256), None, (8, 64, 256),
        (8, 3, 32, 256), (8, 3, 32, 256), (4, 3, 16, 128), (4, 3, 16, 128), (8,) + packed, (8,) + packed,
        (8,) + packed, (6, 8, 2, 16, 128),
        (8,) + packed, (8,) + packed, (8,) + packed,
        (8,) + packed, (8,) + packed, (8,) + packed,
        (4, 3, 16, 128), (4, 3, 16, 128), (8, 3, 32, 256),
        (8, 64, 256), (8, 64, 256), (8, 64, 256),
        (8, 64, 256), (8, 64, 256), (8, 64, 256),
        (8,) + packed, (4, 8) + packed,
    ]
    scratch = [
        pltpu.VMEM((64, 256), F32) if shape is None else pltpu.VMEM(shape, BF16) for shape in shapes
    ]
    scratch += [
        pltpu.VMEM((4, 1, 24), jnp.int32),
        pltpu.SMEM((4, 1, 24), jnp.int32),
        pltpu.SemaphoreType.DMA((6,)),
        pltpu.SemaphoreType.DMA((TRANSFERS, 8)),
        pltpu.SemaphoreType.DMA((TRANSFERS, 8)),
    ]
    child_x, root_x = pl.pallas_call(
        kernel,
        out_shape=(
            jax.ShapeDtypeStruct((8, 64, 256), BF16),
            jax.ShapeDtypeStruct((6, 256, 256), BF16),
        ),
        in_specs=[away] * 5 + [near],
        out_specs=(near, near),
        scratch_shapes=scratch,
        compiler_params=pltpu.CompilerParams(
            collective_id=0, has_side_effects=True, vmem_limit_bytes=40 * 1024 * 1024
        ),
        cost_estimate=pl.CostEstimate(flops=3_000_000_000, bytes_accessed=10_000_000, transcendentals=0),
        name="substitution",
    )(child, rhs, link, root, root_rhs[:, 0], structure)
    child_x = child_x.reshape(2, 256, 256).astype(F32)
    return child_x[None, :, None], root_x.astype(F32)[:, None]


def solution(mesh):
    placed = (
        P("leaf", None, "col", None, None),
        P("leaf", None, "row", None, None, "col", None),
        P(None, "row", None, None, "col", None),
        P("leaf", None, "row", None, None, "col", None),
        P(None, "col", None, None),
        P("leaf", None),
    )
    return jax.shard_map(
        on_device,
        mesh=mesh,
        in_specs=placed,
        out_specs=(P("leaf", None, "col", None, None), P(None, "col", None, None)),
        check_vma=False,
    )
```

time: 1010 us -> 129 us (0.13)
  waiting for transfers between devices: 803 us -> 0 us
  Pallas kernels: 0 us -> 118 us
  other arithmetic: 93 us -> 2.11 us
  blocking collectives: 54.8 us -> 0 us
  matrix products: 22.6 us -> 0 us
  between operations: 14.3 us -> 0.65 us
    reduce_scatter x1 -> x0, waiting for transfers between devices: 403 us -> none  [on_device(): lax.psum_scatter(dense_term, ('leaf', 'row', 'col'), scatter_dimension=0,...]
    psum x4 -> x0, waiting for transfers between devices: 270 us -> none  [the longest x1 73.2 us: on_device(): root_x = lax.psum(x_partial, 'row')]
    all_gather x2 -> x0, waiting for transfers between devices: 129 us -> none  [the longest x1 78.2 us: on_device(): lax.all_gather(my_piece, ('leaf', 'row'), axis=0, tiled=True)]
    pallas_call x0 -> x1, Pallas kernels: none -> 118 us  [on_device(): pl.pallas_call(kernel, out_shape=(jax.ShapeDtypeStruct((8, 64, 256), BF16...]
    add x1 -> x0, other arithmetic: 87.3 us -> none  [on_device(): dense_term + jnp.where(hit[:, :, None, None], lifted[link][None, None], 0.0)]
    psum x1 -> x0, blocking collectives: 54.8 us -> none  [on_device(): root_y = lax.psum(y_partial, 'col').astype(jnp.bfloat16)]
    dot_general x7 -> x0, matrix products: 22.6 us -> none  [the longest x1 6.47 us: on_device(): jnp.einsum('mr,rcn->mcn', choose, whole_root, preferred_element_type=jnp....]
  transfers between devices with their start and end apart: 7 -> 0, of which waited for: 7 -> 0; matrix products, arithmetic and copies ran while one was open for 1% -> 0% of each run, Pallas kernels for 0% -> 0%
where the time goes in v1:
time: 129 us; the launch traced here: 128 us
  Pallas kernels  118 us (91%)
  local copies, waits for them, and re-layouts  7.32 us (6%)
  other arithmetic  2.11 us (2%)
    pallas_call x1, Pallas kernels, on_device(): pl.pallas_call(kernel, out_shape=(jax.ShapeDtypeStruct((8, 64, 256), BF16...  118 us
    unnamed x11, local copies, waits for them, and re-layouts  7.32 us

profile of v1, /device:TPU:1, one launch (start us, length us, event | category | flops | bytes accessed | tf_op | source)
XLA Modules:
  0.0 128.4 jit_solution(2425672092416720280)
XLA Ops:
  0.6 1.1 copy.12
  1.7 0.0 copy-start
  1.8 2.3 %copy-done = bf16[6,1,256,6,1,256]{5,2,4,3,1,0:T(8,128)(2,1)S(1)} copy-done((bf16[6,1,256,6,1,256]{5,2,4,3,1,0:T(8,128)(2,1)S(1)}, bf16[6,1,256,6,1,256]{5,2,4,3,1,0:T(8,128)(2,1)}, u32[]{:S(2)}) %copy-start) | copy-done | bytes 4718616
  4.1 0.0 copy-start.1
  4.1 1.1 copy-done.1
  5.2 0.0 copy-start.2
  5.2 1.1 copy-done.2
  6.4 0.0 copy-start.3
  6.4 0.9 copy-done.3
  7.3 0.0 copy-start.4
  7.3 0.7 copy-done.4
  8.0 118.3 %substitution.1 = (bf16[8,64,256]{2,1,0:T(8,128)(2,1)S(1)}, bf16[6,256,256]{2,1,0:T(8,128)(2,1)S(1)}) custom-call(bf16[2,2,256,256]{3,2,1,0:T(8,128)(2,1)S(1)} %bitcast.26, bf16[2,256,256]{2,1,0:T(8,128)(2,1)S(1)} %bitcast.31, bf16[2,3,256,256]{3,2,1,0:T(8,128)(2,1)S(1)} %bitcast.29, bf16[36,256,256]{2,1,0:T(8,128)(2,1)S(1)} %bitcast.28, ...), custom_call_target="tpu_custom_call" | custom-call | flops 3000000000 | bytes 10000000 | tf_op jit(solution)/shard_map/substitution/pallas_call | solution.py:292
  126.3 1.3 %bitcast_convert_fusion = f32[6,1,256,256]{3,2,1,0:T(8,128)} fusion(bf16[6,256,256]{2,1,0:T(8,128)(2,1)S(1)} %get-tuple-element.5), kind=kLoop, calls=%fused_computation | loop fusion | flops 393216 | bytes 2359296
  127.6 0.8 convert.3
Async XLA Ops:
  1.7 2.3 %copy-start = (bf16[6,1,256,6,1,256]{5,2,4,3,1,0:T(8,128)(2,1)S(1)}, bf16[6,1,256,6,1,256]{5,2,4,3,1,0:T(8,128)(2,1)}, u32[]{:S(2)}) copy-start(bf16[6,1,256,6,1,256]{5,2,4,3,1,0:T(8,128)(2,1)} %param.8) | copy-start | bytes 14155780
  4.1 1.1 copy-start.1
  5.2 1.1 copy-start.2
  6.4 0.9 copy-start.3
  7.3 0.7 copy-start.4

commit v2 on v1

--- a/solution.py
+++ b/solution.py
@@ -9,9 +9,10 @@
 BF16 = jnp.bfloat16
 MESH = pl.DeviceIdType.MESH
 
-(F_RS, F_AG, L_RS, L_X, L_C, U_AG, Y_RS, Y_AG, X_RS, X_C, N_X, N_AG, C_RS, A_AG, D_RS, D_AG,
- S_X, O_AG, O_X) = range(19)
-TRANSFERS = 19
+F_RS, F_AG, L_RS, N_AG, C_RS, A_AG, D_RS, D_AG = range(0, 16, 2)
+L_X, L_C, U_AG, Y_RS, Y_AG, X_RS, X_C, N_X, S_X, O_AG, O_X = range(16, 27)
+TRANSFERS = 27
+HALVES = (0, 1)
 
 
 def swap_halves(v):
@@ -30,11 +31,11 @@
 
 def kernel(
     child_h, rhs_h, link_h, root_h, root_rhs_h, structure_ref,
-    child_out, root_out,
+    child_out_h, root_out_h,
     child, rhs, link, root, root_rhs, child_t, link_t, root_t,
     f_send, f_recv, f_mine, f_all, l_send, l_recv, lx_send, lx_all, c_send, c_recv,
     u_all, spread, y_send, y_recv, y_all, x_send, x_recv, x_all, n_send, n_recv, n_all,
-    c2_send, c2_recv, a_all, d_send, d_recv, d_all, o_all, o_recv,
+    c2_send, c2_recv, a_all, d_send, d_recv, d_all, o_all, o_recv, child_out, root_out,
     ids_v, ids, local_sem, send_sem, recv_sem,
 ):
     leaf, row, col = (lax.axis_index(a) for a in ("leaf", "row", "col"))
@@ -101,31 +102,36 @@
 
     loads[0].wait()
     loads[1].wait()
-    for a in range(2):
-        part = dot(child[a, 0], rhs[0]) + dot(child[a, 1], rhs[1])
-        f_send[pl.ds(4 * a, 4)] = part.reshape(4, 64, 256).astype(BF16)
-    copies = scatter(F_RS, "col", f_send, f_recv)
+    flight = {}
+    for h in HALVES:
+        lanes = slice(128 * h, 128 * h + 128)
+        for a in range(2):
+            part = dot(child[a, 0], rhs[0, :, lanes]) + dot(child[a, 1], rhs[1, :, lanes])
+            f_send[h, pl.ds(4 * a, 4)] = part.reshape(4, 64, 128).astype(BF16)
+        flight[h] = scatter(F_RS + h, "col", f_send.at[h], f_recv.at[h])
     loads[2].wait()
     for a in range(2):
         for m in range(3):
             link_t[m, a] = link[a, m].T
-    arrived(copies)
-    f_mine[...] = total("col", f_send, f_recv)
-    f_all[col] = f_mine[...].astype(BF16)
-    copies = gather(F_AG, "col", f_all)
+    for h in HALVES:
+        arrived(flight[h])
+        f_mine[h] = total("col", f_send.at[h], f_recv.at[h])
+        f_all[h, col] = f_mine[h].astype(BF16)
+        flight[h] = gather(F_AG + h, "col", f_all.at[h])
     for a in range(2):
         for x in range(2):
             child_t[x, a] = child[a, x].T
+
+    for h in HALVES:
+        arrived(flight[h])
+        for m in range(3):
+            part = jnp.zeros((256, 128), F32)
+            for a in range(2):
+                part = part + dot(link_t[m, a], f_all[h, pl.ds(4 * a, 4)].reshape(256, 128))
+            l_send[h, :, m] = part.reshape(8, 32, 128).astype(BF16)
+        flight[h] = scatter(L_RS + h, "row", l_send.at[h], l_recv.at[h])
     loads[3].wait()
     loads[4].wait()
-    arrived(copies)
-
-    for m in range(3):
-        part = jnp.zeros((256, 256), F32)
-        for a in range(2):
-            part = part + dot(link_t[m, a], f_all[pl.ds(4 * a, 4)].reshape(256, 256))
-        l_send[:, m] = part.reshape(8, 32, 256).astype(BF16)
-    copies = scatter(L_RS, "row", l_send, l_recv)
 
     def turn(n, carry):
         a, x = n // 6, n % 6
@@ -137,11 +143,10 @@
     to_scalars = pltpu.make_async_copy(ids_v, ids, local_sem.at[5])
     to_scalars.start()
     to_scalars.wait()
-    arrived(copies)
-    lifted = total("row", l_send, l_recv)
-    for h in range(2):
-        lanes = lifted[:, :, 128 * h : 128 * h + 128]
-        for q, packed in enumerate(pack_quarters(lanes[:, :16], lanes[:, 16:])):
+    for h in HALVES:
+        arrived(flight[h])
+        lifted = total("row", l_send.at[h], l_recv.at[h])
+        for q, packed in enumerate(pack_quarters(lifted[:, :16], lifted[:, 16:])):
             lx_send[2 * h + q] = packed.astype(BF16)
     copies = start(L_X, "leaf", lambda there: lx_send.at[there], lambda step: lx_all.at[leaf])
     lx_all[leaf] = lx_send[leaf]
@@ -216,44 +221,55 @@
         return top.astype(BF16), bottom.astype(BF16)
 
     arrived(copies)
-    for h in range(2):
+    for h in HALVES:
         top, bottom = unpack(n_recv[2 * h], n_recv[2 * h + 1])
-        n_all[row, :, pl.ds(0, 16), pl.ds(128 * h, 128)] = top
-        n_all[row, :, pl.ds(16, 16), pl.ds(128 * h, 128)] = bottom
-    copies = gather(N_AG, "row", n_all)
-    arrived(copies)
-
-    for a in range(2):
-        part = jnp.zeros((256, 256), F32)
-        for m in range(3):
-            part = part + dot(link[a, m], n_all[:, m].reshape(256, 256))
-        c2_send[pl.ds(4 * a, 4)] = part.reshape(4, 64, 256).astype(BF16)
-    copies = scatter(C_RS, "col", c2_send, c2_recv)
+        n_all[h, row, :, pl.ds(0, 16)] = top
+        n_all[h, row, :, pl.ds(16, 16)] = bottom
+        flight[h] = gather(N_AG + h, "row", n_all.at[h])
+
+    for h in HALVES:
+        arrived(flight[h])
+        for a in range(2):
+            part = jnp.zeros((256, 128), F32)
+            for m in range(3):
+                part = part + dot(link[a, m], n_all[h, :, m].reshape(256, 128))
+            c2_send[h, pl.ds(4 * a, 4)] = part.reshape(4, 64, 128).astype(BF16)
+        flight[h] = scatter(C_RS + h, "col", c2_send.at[h], c2_recv.at[h])
     arrived(out_copies)
     o_recv[leaf] = o_all[...]
     out_copies = start(O_X, "leaf", lambda there: o_all, lambda step: o_recv.at[leaf])
-    arrived(copies)
-    a_all[col] = (f_mine[...] - total("col", c2_send, c2_recv)).astype(BF16)
-    copies = gather(A_AG, "col", a_all)
-    arrived(copies)
-
-    for x in range(2):
-        part = jnp.zeros((256, 256), F32)
-        for a in range(2):
-            part = part + dot(child_t[x, a], a_all[pl.ds(4 * a, 4)].reshape(256, 256))
-        d_send[pl.ds(4 * x, 4)] = part.reshape(4, 64, 256).astype(BF16)
-    copies = scatter(D_RS, "row", d_send, d_recv)
+    for h in HALVES:
+        arrived(flight[h])
+        a_all[h, col] = (f_mine[h] - total("col", c2_send.at[h], c2_recv.at[h])).astype(BF16)
+        flight[h] = gather(A_AG + h, "col", a_all.at[h])
+
+    for h in HALVES:
+        arrived(flight[h])
+        for x in range(2):
+            part = jnp.zeros((256, 128), F32)
+            for a in range(2):
+                part = part + dot(child_t[x, a], a_all[h, pl.ds(4 * a, 4)].reshape(256, 128))
+            d_send[h, pl.ds(4 * x, 4)] = part.reshape(4, 64, 128).astype(BF16)
+        flight[h] = scatter(D_RS + h, "row", d_send.at[h], d_recv.at[h])
+    for h in HALVES:
+        arrived(flight[h])
+        d_all[h, row] = total("row", d_send.at[h], d_recv.at[h]).astype(BF16)
+        flight[h] = gather(D_AG + h, "row", d_all.at[h])
     arrived(out_copies)
-    for h in range(2):
+    for h in HALVES:
         for r in range(8):
             top, bottom = unpack(o_recv[2 * h, r], o_recv[2 * h + 1, r])
             root_out[:, pl.ds(32 * r, 16), pl.ds(128 * h, 128)] = top
             root_out[:, pl.ds(32 * r + 16, 16), pl.ds(128 * h, 128)] = bottom
-    arrived(copies)
-    d_all[row] = total("row", d_send, d_recv).astype(BF16)
-    copies = gather(D_AG, "row", d_all)
-    arrived(copies)
-    child_out[...] = d_all[...]
+    root_store = pltpu.make_async_copy(root_out, root_out_h, local_sem.at[6])
+    root_store.start()
+    for h in HALVES:
+        arrived(flight[h])
+        child_out[:, :, pl.ds(128 * h, 128)] = d_all[h]
+    child_store = pltpu.make_async_copy(child_out, child_out_h, local_sem.at[7])
+    child_store.start()
+    child_store.wait()
+    root_store.wait()
     for copy in started:
         copy.wait_send()
 
@@ -263,29 +279,30 @@
     rhs = child_rhs[0, :, 0]
     link = coupling[0, :, 0, :, :, 0, :].transpose(0, 2, 1, 3)
     root = root_inv[:, 0, :, :, 0, :].transpose(0, 2, 1, 3).reshape(36, 256, 256)
-    away = pl.BlockSpec(memory_space=pl.ANY)
+    away = pl.BlockSpec(memory_space=pltpu.HBM)
     near = pl.BlockSpec(memory_space=pltpu.VMEM)
     packed = (6, 16, 128)
+    half = (2, 8, 64, 128)
     shapes = [
         (2, 2, 256, 256), (2, 256, 256), (2, 3, 256, 256), (36, 256, 256), (6, 256, 256),
         (2, 2, 256, 256), (3, 2, 256, 256), (36, 256, 256),
-        (8, 64, 256), (8, 64, 256), None, (8, 64, 256),
-        (8, 3, 32, 256), (8, 3, 32, 256), (4, 3, 16, 128), (4, 3, 16, 128), (8,) + packed, (8,) + packed,
+        half, half, None, half,
+        (2, 8, 3, 32, 128), (2, 8, 3, 32, 128), (4, 3, 16, 128), (4, 3, 16, 128), (8,) + packed, (8,) + packed,
         (8,) + packed, (6, 8, 2, 16, 128),
         (8,) + packed, (8,) + packed, (8,) + packed,
         (8,) + packed, (8,) + packed, (8,) + packed,
-        (4, 3, 16, 128), (4, 3, 16, 128), (8, 3, 32, 256),
-        (8, 64, 256), (8, 64, 256), (8, 64, 256),
-        (8, 64, 256), (8, 64, 256), (8, 64, 256),
-        (8,) + packed, (4, 8) + packed,
+        (4, 3, 16, 128), (4, 3, 16, 128), (2, 8, 3, 32, 128),
+        half, half, half,
+        half, half, half,
+        (8,) + packed, (4, 8) + packed, (8, 64, 256), (6, 256, 256),
     ]
     scratch = [
-        pltpu.VMEM((64, 256), F32) if shape is None else pltpu.VMEM(shape, BF16) for shape in shapes
+        pltpu.VMEM((2, 64, 128), F32) if shape is None else pltpu.VMEM(shape, BF16) for shape in shapes
     ]
     scratch += [
         pltpu.VMEM((4, 1, 24), jnp.int32),
         pltpu.SMEM((4, 1, 24), jnp.int32),
-        pltpu.SemaphoreType.DMA((6,)),
+        pltpu.SemaphoreType.DMA((8,)),
         pltpu.SemaphoreType.DMA((TRANSFERS, 8)),
         pltpu.SemaphoreType.DMA((TRANSFERS, 8)),
     ]
@@ -296,10 +313,10 @@
             jax.ShapeDtypeStruct((6, 256, 256), BF16),
         ),
         in_specs=[away] * 5 + [near],
-        out_specs=(near, near),
+        out_specs=(away, away),
         scratch_shapes=scratch,
         compiler_params=pltpu.CompilerParams(
-            collective_id=0, has_side_effects=True, vmem_limit_bytes=40 * 1024 * 1024
+            collective_id=0, has_side_effects=True, vmem_limit_bytes=60 * 1024 * 1024
         ),
         cost_estimate=pl.CostEstimate(flops=3_000_000_000, bytes_accessed=10_000_000, transcendentals=0),
         name="substitution",

time: 129 us -> 117 us (0.907)
  Pallas kernels: 118 us -> 111 us
  local copies, waits for them, and re-layouts: 7.32 us -> 1.91 us
    pallas_call x1, Pallas kernels: 118 us -> 111 us  [on_device(): pl.pallas_call(kernel, out_shape=(jax.ShapeDtypeStruct((8, 64, 256), BF16...]
    unnamed x11 -> x3, local copies, waits for them, and re-layouts: 7.32 us -> 1.91 us
where the time goes in v2:
time: 117 us
  Pallas kernels  111 us (95%)
  other arithmetic  3.29 us (3%)
  local copies, waits for them, and re-layouts  1.91 us (2%)
    pallas_call x1, Pallas kernels, on_device(): pl.pallas_call(kernel, out_shape=(jax.ShapeDtypeStruct((8, 64, 256), BF16...  111 us
    unnamed x2, other arithmetic  3.29 us

profile of v2, /device:TPU:1, one launch (start us, length us, event | category | flops | bytes accessed | tf_op | source)
XLA Modules:
  0.0 117.0 jit_solution(18096662067234012929)
XLA Ops:
  0.6 1.9 %copy.12 = bf16[1,2,1,256,2,1,256]{6,3,4,1,5,2,0:T(8,128)(2,1)} copy(bf16[1,2,1,256,2,1,256]{6,4,5,3,2,1,0:T(2,128)(2,1)} %param.7) | data formatting | bytes 1048576 | tf_op args[1]
  2.5 111.2 %substitution.1 = (bf16[8,64,256]{2,1,0:T(8,128)(2,1)}, bf16[6,256,256]{2,1,0:T(8,128)(2,1)}) custom-call(bf16[2,2,256,256]{3,2,1,0:T(8,128)(2,1)} %bitcast.26, bf16[2,256,256]{2,1,0:T(8,128)(2,1)} %bitcast.31, bf16[2,3,256,256]{3,2,1,0:T(8,128)(2,1)} %bitcast.29, bf16[36,256,256]{2,1,0:T(8,128)(2,1)} %bitcast.28, bf16[6,256,256]{2,1,0:T(8,128)(2,1)} %bitcast.30, ...), custom_call_target="tpu_custom_call" | custom-call | flops 3000000000 | bytes 10000000 | tf_op jit(solution)/shard_map/substitution/pallas_call | solution.py:309
  113.7 0.0 copy-start
  113.7 2.5 %bitcast_convert_fusion = f32[6,1,256,256]{3,2,1,0:T(8,128)} fusion(bf16[6,256,256]{2,1,0:T(8,128)(2,1)} %get-tuple-element.5), kind=kLoop, calls=%fused_computation | loop fusion | flops 393216 | bytes 2359296
  116.2 0.0 copy-done
  116.2 0.8 convert.3
Async XLA Ops:
  113.7 2.5 %copy-start = (bf16[8,64,256]{2,1,0:T(8,128)(2,1)S(1)}, bf16[8,64,256]{2,1,0:T(8,128)(2,1)}, u32[]{:S(2)}) copy-start(bf16[8,64,256]{2,1,0:T(8,128)(2,1)} %get-tuple-element.4) | copy-start | bytes 786436

commit v3 on v2

v3 whole, which is shorter than its diff:
```python
import jax
import jax.numpy as jnp
from jax import lax
from jax.experimental import pallas as pl
from jax.experimental.pallas import tpu as pltpu
from jax.sharding import PartitionSpec as P

F32 = jnp.float32
BF16 = jnp.bfloat16
MESH = pl.DeviceIdType.MESH

N_XZ, C_RS, A_AG, D_RS, D_AG = range(0, 10, 2)
F_RS, F_AG, L_XZ, L_C, U_AG, Y_RS, Y_AG, X_RS, X_C, S_X, O_AG, O_X = range(10, 22)
TRANSFERS = 22
HALVES = (0, 1)
FAR_FIRST = (4, 3, 5, 2, 6, 1, 7)


def swap_halves(v):
    flat = v.reshape(-1, 128)
    return pltpu.roll(flat, 64, 1).reshape(v.shape)


def left_half(shape):
    return lax.broadcasted_iota(jnp.int32, shape, len(shape) - 1) < 64


def pack_quarters(top, bottom):
    left = left_half(top.shape)
    return jnp.where(left, top, swap_halves(bottom)), jnp.where(left, swap_halves(top), bottom)


def kernel(
    child_h, rhs_h, link_h, root_h, root_rhs_h, structure_ref,
    child_out_h, root_out_h,
    child, rhs, link, root, root_rhs, child_t, link_t, root_t,
    f_send, f_recv, f_mine, f_all, l_send, l_recv, lx_all, c_send, c_recv,
    u_all, spread, y_send, y_recv, y_all, x_send, x_recv, x_all, n_send, n_recv, n_all,
    c2_send, c2_recv, a_all, d_send, d_recv, d_all, o_all, o_recv, child_out, root_out,
    ids_v, ids, local_sem, send_sem, recv_sem,
):
    leaf, row, col = (lax.axis_index(a) for a in ("leaf", "row", "col"))
    place = {"leaf": leaf, "row": row, "col": col}
    size = {"leaf": 4, "row": 8, "col": 8}
    sends = []

    def peer(axis, step):
        return lax.rem(place[axis] + step, size[axis])

    def copy(number, arrival, source, target, device):
        return pltpu.make_async_remote_copy(
            src_ref=source, dst_ref=target,
            send_sem=send_sem.at[number], recv_sem=recv_sem.at[arrival],
            device_id=device, device_id_type=MESH,
        )

    def start(number, axis, source, target, whole):
        for step in FAR_FIRST if size[axis] == 8 else (2, 1, 3):
            there = peer(axis, step)
            copy(number, number, source(there), target(step), {axis: there}).start()
        pending = copy(number, number, whole, whole, {axis: peer(axis, 1)})
        sends.append(pending)
        return pending

    def scatter(number, axis, parts, landing):
        return start(
            number, axis, lambda there: parts.at[there], lambda step: landing.at[step], parts.at[pl.ds(0, size[axis] - 1)]
        )

    def gather(number, axis, whole):
        mine = whole.at[place[axis]]
        return start(number, axis, lambda there: mine, lambda step: mine, whole.at[pl.ds(0, size[axis] - 1)])

    def arrived(pending):
        pending.wait_recv()

    def total(axis, parts, landing):
        value = parts[place[axis]].astype(F32)
        for step in range(1, size[axis]):
            value = value + landing[step].astype(F32)
        return value

    def dot(a, b):
        return jnp.dot(a, b, preferred_element_type=F32)

    loads = [
        pltpu.make_async_copy(src, dst, local_sem.at[n])
        for n, (src, dst) in enumerate(
            ((child_h, child), (rhs_h, rhs), (link_h, link), (root_rhs_h, root_rhs), (root_h, root))
        )
    ]
    loads[0].start()
    loads[1].start()
    barrier = pltpu.get_barrier_semaphore()
    for step in range(1, 8):
        pl.semaphore_signal(barrier, inc=1, device_id={"col": peer("col", step)}, device_id_type=MESH)
    for step in range(1, 32):
        there = {"leaf": peer("leaf", step // 8), "row": peer("row", step % 8)}
        pl.semaphore_signal(barrier, inc=1, device_id=there, device_id_type=MESH)
    ids_v[leaf] = structure_ref[...]

    loads[0].wait()
    loads[1].wait()
    for a in range(2):
        part = dot(child[a, 0], rhs[0]) + dot(child[a, 1], rhs[1])
        f_send[pl.ds(4 * a, 4)] = part.reshape(4, 64, 256).astype(BF16)
    pl.semaphore_wait(barrier, 38)
    pending = scatter(F_RS, "col", f_send, f_recv)
    for load in loads[2:]:
        load.start()
    structure_pending = start(
        S_X, "leaf", lambda there: structure_ref, lambda step: ids_v.at[leaf], ids_v.at[pl.ds(0, 3)]
    )
    loads[2].wait()
    for a in range(2):
        for m in range(3):
            link_t[m, a] = link[a, m].T
    arrived(pending)
    f_mine[...] = total("col", f_send, f_recv)
    f_all[col] = f_mine[...].astype(BF16)
    pending = gather(F_AG, "col", f_all)
    for a in range(2):
        for x in range(2):
            child_t[x, a] = child[a, x].T
    arrived(pending)

    for h in HALVES:
        for m in range(3):
            part = jnp.zeros((256, 128), F32)
            for a in range(2):
                part = part + dot(link_t[m, a], f_all[pl.ds(4 * a, 4), :, pl.ds(128 * h, 128)].reshape(256, 128))
            part = part.reshape(8, 2, 16, 128)
            for q, packed in enumerate(pack_quarters(part[:, 0], part[:, 1])):
                l_send[2 * h + q, :, m] = packed.astype(BF16)
        for step in FAR_FIRST:
            for there in (2 * h, 2 * h + 1):
                at = peer("row", step)
                copy(L_XZ, L_XZ, l_send.at[there, at], l_recv.at[leaf * 8 + step], {"leaf": there, "row": at}).start()
    for step in (2, 1, 3):
        there = peer("leaf", step)
        copy(L_XZ, L_XZ, l_send.at[there, row], l_recv.at[leaf * 8], {"leaf": there}).start()
    pltpu.make_async_copy(l_send.at[leaf, row], l_recv.at[leaf * 8], recv_sem.at[L_XZ]).start()
    pending = copy(L_XZ, L_XZ, l_recv.at[pl.ds(0, 31)], l_recv, {"row": peer("row", 1)})
    sends.append(pending)
    loads[3].wait()
    loads[4].wait()

    def turn(n, carry):
        a, x = n // 6, n % 6
        root_t[x * 6 + a] = root[a * 6 + x].T
        return carry

    lax.fori_loop(0, 36, turn, 0)
    arrived(structure_pending)
    to_scalars = pltpu.make_async_copy(ids_v, ids, local_sem.at[5])
    to_scalars.start()
    to_scalars.wait()
    arrived(pending)
    for child_at in range(4):
        value = l_recv[child_at * 8].astype(F32)
        for step in range(1, 8):
            value = value + l_recv[child_at * 8 + step].astype(F32)
        lx_all[child_at] = value

    block = lax.broadcasted_iota(jnp.int32, (6, 16, 128), 0) * 8
    for target in range(8):
        value = jnp.zeros((6, 16, 128), F32)
        for child_at in range(4):
            for m in range(3):
                wanted = ids[child_at, 0, col + 8 * m] - target
                value = value + jnp.where(block == wanted, lx_all[child_at, m][None], 0.0)
        c_send[target] = value.astype(BF16)
    pending = scatter(L_C, "col", c_send, c_recv)
    base = root_rhs[:, pl.ds(pl.multiple_of(row * 32, 32), 32), pl.ds(pl.multiple_of((leaf // 2) * 128, 128), 128)]
    base = base.astype(F32)
    first, second = pack_quarters(base[:, :16], base[:, 16:])
    base = jnp.where(leaf % 2 == 0, first, second)
    arrived(pending)
    u_all[row] = (base - total("col", c_send, c_recv)).astype(BF16)
    pending = gather(U_AG, "row", u_all)
    left = left_half((8, 16, 128))
    keep_left = jnp.where(left, 1.0, 0.0).astype(BF16)
    keep_right = jnp.where(left, 0.0, 1.0).astype(BF16)

    def spread_out(whole):
        for a in range(6):
            spread[a, :, 0] = whole[:, a] * keep_left
            spread[a, :, 1] = whole[:, a] * keep_right

    def root_product(matrix, parts):
        for a in range(6):
            value = jnp.zeros((256, 128), F32)
            for x in range(6):
                value = value + dot(matrix[a * 6 + x], spread[x].reshape(256, 128))
            value = value + swap_halves(value)
            value = value.reshape(8, 2, 16, 128)
            parts[:, a] = jnp.where(left, value[:, 0], value[:, 1]).astype(BF16)

    arrived(pending)
    spread_out(u_all)
    root_product(root, y_send)
    pending = scatter(Y_RS, "col", y_send, y_recv)
    arrived(pending)
    y_all[col] = total("col", y_send, y_recv).astype(BF16)
    pending = gather(Y_AG, "col", y_all)
    arrived(pending)
    spread_out(y_all)
    root_product(root_t, x_send)
    pending = scatter(X_RS, "row", x_send, x_recv)
    arrived(pending)
    solved = total("row", x_send, x_recv).astype(BF16)
    x_all[col] = solved
    pending = gather(X_C, "col", x_all)
    o_all[row] = solved
    arrived(pending)

    for child_at in range(4):
        for m in range(3):
            r = ids[child_at, 0, col + 8 * m]
            n_send[child_at, m] = x_all[r & 7, r >> 3]
    half_at = N_XZ + leaf // 2
    for step in FAR_FIRST + (0,):
        for leaf_step in (0, 1, 2, 3) if step else (1, 2, 3):
            there, at = peer("leaf", leaf_step), peer("row", step)
            copy(N_XZ, half_at, n_send.at[there], n_recv.at[leaf, row], {"leaf": there, "row": at}).start()
    pltpu.make_async_copy(n_send.at[leaf], n_recv.at[leaf, row], recv_sem.at[half_at]).start()
    sends.append(copy(N_XZ, N_XZ, l_recv.at[pl.ds(0, 31)], l_recv, {"row": peer("row", 1)}))
    out_pending = gather(O_AG, "row", o_all)

    def unpack(even, odd):
        even, odd = even.astype(F32), odd.astype(F32)
        mask = left_half(even.shape)
        top = jnp.where(mask, even, swap_halves(odd))
        bottom = jnp.where(mask, swap_halves(even), odd)
        return top.astype(BF16), bottom.astype(BF16)

    flight = {}
    for h in HALVES:
        pieces = n_recv.at[pl.ds(2 * h, 2)]
        arrived(copy(N_XZ, N_XZ + h, pieces, pieces, {"row": peer("row", 1)}))
        for m in range(3):
            n_all[m, :, 0], n_all[m, :, 1] = unpack(n_recv[2 * h, :, m], n_recv[2 * h + 1, :, m])
        for a in range(2):
            part = jnp.zeros((256, 128), F32)
            for m in range(3):
                part = part + dot(link[a, m], n_all[m].reshape(256, 128))
            c2_send[h, pl.ds(4 * a, 4)] = part.reshape(4, 64, 128).astype(BF16)
        flight[h] = scatter(C_RS + h, "col", c2_send.at[h], c2_recv.at[h])
    for h in HALVES:
        arrived(flight[h])
        carried = total("col", c2_send.at[h], c2_recv.at[h])
        a_all[h, col] = (f_mine[:, pl.ds(128 * h, 128)] - carried).astype(BF16)
        flight[h] = gather(A_AG + h, "col", a_all.at[h])
    arrived(out_pending)
    o_recv[leaf] = o_all[...]
    out_pending = start(O_X, "leaf", lambda there: o_all, lambda step: o_recv.at[leaf], o_recv.at[pl.ds(0, 3)])

    for h in HALVES:
        arrived(flight[h])
        for x in range(2):
            part = jnp.zeros((256, 128), F32)
            for a in range(2):
                part = part + dot(child_t[x, a], a_all[h, pl.ds(4 * a, 4)].reshape(256, 128))
            d_send[h, pl.ds(4 * x, 4)] = part.reshape(4, 64, 128).astype(BF16)
        flight[h] = scatter(D_RS + h, "row", d_send.at[h], d_recv.at[h])
    for h in HALVES:
        arrived(flight[h])
        d_all[h, row] = total("row", d_send.at[h], d_recv.at[h]).astype(BF16)
        flight[h] = gather(D_AG + h, "row", d_all.at[h])
    arrived(out_pending)
    for h in HALVES:
        for r in range(8):
            top, bottom = unpack(o_recv[2 * h, r], o_recv[2 * h + 1, r])
            root_out[:, pl.ds(32 * r, 16), pl.ds(128 * h, 128)] = top
            root_out[:, pl.ds(32 * r + 16, 16), pl.ds(128 * h, 128)] = bottom
    root_store = pltpu.make_async_copy(root_out, root_out_h, local_sem.at[6])
    root_store.start()
    for h in HALVES:
        arrived(flight[h])
        child_out[:, :, pl.ds(128 * h, 128)] = d_all[h]
    child_store = pltpu.make_async_copy(child_out, child_out_h, local_sem.at[7])
    child_store.start()
    child_store.wait()
    root_store.wait()
    for pending in sends:
        pending.wait_send()


def on_device(child_rhs, child_inv, root_inv, coupling, root_rhs, structure):
    child = child_inv[0, :, 0, :, :, 0, :].transpose(0, 2, 1, 3)
    rhs = child_rhs[0, :, 0]
    link = coupling[0, :, 0, :, :, 0, :].transpose(0, 2, 1, 3)
    root = root_inv[:, 0, :, :, 0, :].transpose(0, 2, 1, 3).reshape(36, 256, 256)
    away = pl.BlockSpec(memory_space=pltpu.HBM)
    near = pl.BlockSpec(memory_space=pltpu.VMEM)
    packed = (6, 16, 128)
    half = (2, 8, 64, 128)
    shapes = [
        (2, 2, 256, 256), (2, 256, 256), (2, 3, 256, 256), (36, 256, 256), (6, 256, 256),
        (2, 2, 256, 256), (3, 2, 256, 256), (36, 256, 256),
        (8, 64, 256), (8, 64, 256), None, (8, 64, 256),
        (4, 8, 3, 16, 128), (32, 3, 16, 128), None, (8,) + packed, (8,) + packed,
        (8,) + packed, (6, 8, 2, 16, 128),
        (8,) + packed, (8,) + packed, (8,) + packed,
        (8,) + packed, (8,) + packed, (8,) + packed,
        (4, 3, 16, 128), (4, 8, 3, 16, 128), (3, 8, 2, 16, 128),
        half, half, half,
        half, half, half,
        (8,) + packed, (4, 8) + packed, (8, 64, 256), (6, 256, 256),
    ]
    wide = iter([(64, 256), (4, 3, 16, 128)])
    scratch = [
        pltpu.VMEM(next(wide), F32) if shape is None else pltpu.VMEM(shape, BF16) for shape in shapes
    ]
    scratch += [
        pltpu.VMEM((4, 1, 24), jnp.int32),
        pltpu.SMEM((4, 1, 24), jnp.int32),
        pltpu.SemaphoreType.DMA((8,)),
        pltpu.SemaphoreType.DMA((TRANSFERS,)),
        pltpu.SemaphoreType.DMA((TRANSFERS,)),
    ]
    child_x, root_x = pl.pallas_call(
        kernel,
        out_shape=(
            jax.ShapeDtypeStruct((8, 64, 256), BF16),
            jax.ShapeDtypeStruct((6, 256, 256), BF16),
        ),
        in_specs=[away] * 5 + [near],
        out_specs=(away, away),
        scratch_shapes=scratch,
        compiler_params=pltpu.CompilerParams(
            collective_id=0, has_side_effects=True, vmem_limit_bytes=60 * 1024 * 1024
        ),
        cost_estimate=pl.CostEstimate(flops=3_000_000_000, bytes_accessed=10_000_000, transcendentals=0),
        name="substitution",
    )(child, rhs, link, root, root_rhs[:, 0], structure)
    child_x = child_x.reshape(2, 256, 256).astype(F32)
    return child_x[None, :, None], root_x.astype(F32)[:, None]


def solution(mesh):
    placed = (
        P("leaf", None, "col", None, None),
        P("leaf", None, "row", None, None, "col", None),
        P(None, "row", None, None, "col", None),
        P("leaf", None, "row", None, None, "col", None),
        P(None, "col", None, None),
        P("leaf", None),
    )
    return jax.shard_map(
        on_device,
        mesh=mesh,
        in_specs=placed,
        out_specs=(P("leaf", None, "col", None, None), P(None, "col", None, None)),
        check_vma=False,
    )
```

time: 117 us -> 107 us (0.915)
  Pallas kernels: 111 us -> 101 us
    pallas_call x1, Pallas kernels: 111 us -> 101 us  [on_device(): pl.pallas_call(kernel, out_shape=(jax.ShapeDtypeStruct((8, 64, 256), BF16...]
where the time goes in v3:
time: 107 us
  Pallas kernels  101 us (94%)
  other arithmetic  3.29 us (3%)
  local copies, waits for them, and re-layouts  1.91 us (2%)
    pallas_call x1, Pallas kernels, on_device(): pl.pallas_call(kernel, out_shape=(jax.ShapeDtypeStruct((8, 64, 256), BF16...  101 us
    unnamed x2, other arithmetic  3.29 us

profile of v3, /device:TPU:1, one launch (start us, length us, event | category | flops | bytes accessed | tf_op | source)
XLA Modules:
  0.0 106.9 jit_solution(1093192885163795090)
XLA Ops:
  0.6 1.9 %copy.12 = bf16[1,2,1,256,2,1,256]{6,3,4,1,5,2,0:T(8,128)(2,1)} copy(bf16[1,2,1,256,2,1,256]{6,4,5,3,2,1,0:T(2,128)(2,1)} %param.7) | data formatting | bytes 1048576 | tf_op args[1]
  2.5 101.1 %substitution.1 = (bf16[8,64,256]{2,1,0:T(8,128)(2,1)}, bf16[6,256,256]{2,1,0:T(8,128)(2,1)}) custom-call(bf16[2,2,256,256]{3,2,1,0:T(8,128)(2,1)} %bitcast.26, bf16[2,256,256]{2,1,0:T(8,128)(2,1)} %bitcast.31, bf16[2,3,256,256]{3,2,1,0:T(8,128)(2,1)} %bitcast.29, bf16[36,256,256]{2,1,0:T(8,128)(2,1)} %bitcast.28, bf16[6,256,256]{2,1,0:T(8,128)(2,1)} %bitcast.30, ...), custom_call_target="tpu_custom_call" | custom-call | flops 3000000000 | bytes 10000000 | tf_op jit(solution)/shard_map/substitution/pallas_call | solution.py:322
  103.6 0.0 copy-start
  103.6 2.5 %bitcast_convert_fusion = f32[6,1,256,256]{3,2,1,0:T(8,128)} fusion(bf16[6,256,256]{2,1,0:T(8,128)(2,1)} %get-tuple-element.5), kind=kLoop, calls=%fused_computation | loop fusion | flops 393216 | bytes 2359296
  106.1 0.0 copy-done
  106.1 0.8 convert.3
Async XLA Ops:
  103.6 2.5 %copy-start = (bf16[8,64,256]{2,1,0:T(8,128)(2,1)S(1)}, bf16[8,64,256]{2,1,0:T(8,128)(2,1)}, u32[]{:S(2)}) copy-start(bf16[8,64,256]{2,1,0:T(8,128)(2,1)} %get-tuple-element.4) | copy-start | bytes 786436

commit v4 on v3

--- a/solution.py
+++ b/solution.py
@@ -31,12 +31,12 @@
 
 
 def kernel(
-    child_h, rhs_h, link_h, root_h, root_rhs_h, structure_ref,
-    child_out_h, root_out_h,
-    child, rhs, link, root, root_rhs, child_t, link_t, root_t,
+    child, rhs, link_h, root_h, root_rhs_h, structure_h,
+    child_out, root_out,
+    link, root, root_rhs, child_t, link_t, root_t,
     f_send, f_recv, f_mine, f_all, l_send, l_recv, lx_all, c_send, c_recv,
     u_all, spread, y_send, y_recv, y_all, x_send, x_recv, x_all, n_send, n_recv, n_all,
-    c2_send, c2_recv, a_all, d_send, d_recv, d_all, o_all, o_recv, child_out, root_out,
+    c2_send, c2_recv, a_all, d_send, d_recv, d_all, o_all, o_recv,
     ids_v, ids, local_sem, send_sem, recv_sem,
 ):
     leaf, row, col = (lax.axis_index(a) for a in ("leaf", "row", "col"))
@@ -86,32 +86,32 @@
     loads = [
         pltpu.make_async_copy(src, dst, local_sem.at[n])
         for n, (src, dst) in enumerate(
-            ((child_h, child), (rhs_h, rhs), (link_h, link), (root_rhs_h, root_rhs), (root_h, root))
+            (
+                (structure_h, ids_v.at[leaf]), (link_h, link), (root_rhs_h, root_rhs), (root_h, root),
+            )
         )
     ]
     loads[0].start()
-    loads[1].start()
     barrier = pltpu.get_barrier_semaphore()
     for step in range(1, 8):
         pl.semaphore_signal(barrier, inc=1, device_id={"col": peer("col", step)}, device_id_type=MESH)
     for step in range(1, 32):
         there = {"leaf": peer("leaf", step // 8), "row": peer("row", step % 8)}
         pl.semaphore_signal(barrier, inc=1, device_id=there, device_id_type=MESH)
-    ids_v[leaf] = structure_ref[...]
-
-    loads[0].wait()
-    loads[1].wait()
+
     for a in range(2):
         part = dot(child[a, 0], rhs[0]) + dot(child[a, 1], rhs[1])
         f_send[pl.ds(4 * a, 4)] = part.reshape(4, 64, 256).astype(BF16)
     pl.semaphore_wait(barrier, 38)
     pending = scatter(F_RS, "col", f_send, f_recv)
-    for load in loads[2:]:
+    for load in loads[1:]:
         load.start()
+    loads[0].wait()
+    mine = ids_v.at[leaf]
     structure_pending = start(
-        S_X, "leaf", lambda there: structure_ref, lambda step: ids_v.at[leaf], ids_v.at[pl.ds(0, 3)]
+        S_X, "leaf", lambda there: structure_h, lambda step: ids_v.at[leaf], ids_v.at[pl.ds(0, 3)]
     )
-    loads[2].wait()
+    loads[1].wait()
     for a in range(2):
         for m in range(3):
             link_t[m, a] = link[a, m].T
@@ -142,17 +142,17 @@
     pltpu.make_async_copy(l_send.at[leaf, row], l_recv.at[leaf * 8], recv_sem.at[L_XZ]).start()
     pending = copy(L_XZ, L_XZ, l_recv.at[pl.ds(0, 31)], l_recv, {"row": peer("row", 1)})
     sends.append(pending)
+    loads[2].wait()
     loads[3].wait()
-    loads[4].wait()
 
     def turn(n, carry):
         a, x = n // 6, n % 6
         root_t[x * 6 + a] = root[a * 6 + x].T
         return carry
 
-    lax.fori_loop(0, 36, turn, 0)
+    lax.fori_loop(0, 12, turn, 0)
     arrived(structure_pending)
-    to_scalars = pltpu.make_async_copy(ids_v, ids, local_sem.at[5])
+    to_scalars = pltpu.make_async_copy(ids_v, ids, local_sem.at[6])
     to_scalars.start()
     to_scalars.wait()
     arrived(pending)
@@ -178,6 +178,7 @@
     arrived(pending)
     u_all[row] = (base - total("col", c_send, c_recv)).astype(BF16)
     pending = gather(U_AG, "row", u_all)
+    lax.fori_loop(12, 36, turn, 0)
     left = left_half((8, 16, 128))
     keep_left = jnp.where(left, 1.0, 0.0).astype(BF16)
     keep_right = jnp.where(left, 0.0, 1.0).astype(BF16)
@@ -225,7 +226,6 @@
             copy(N_XZ, half_at, n_send.at[there], n_recv.at[leaf, row], {"leaf": there, "row": at}).start()
     pltpu.make_async_copy(n_send.at[leaf], n_recv.at[leaf, row], recv_sem.at[half_at]).start()
     sends.append(copy(N_XZ, N_XZ, l_recv.at[pl.ds(0, 31)], l_recv, {"row": peer("row", 1)}))
-    out_pending = gather(O_AG, "row", o_all)
 
     def unpack(even, odd):
         even, odd = even.astype(F32), odd.astype(F32)
@@ -246,14 +246,12 @@
                 part = part + dot(link[a, m], n_all[m].reshape(256, 128))
             c2_send[h, pl.ds(4 * a, 4)] = part.reshape(4, 64, 128).astype(BF16)
         flight[h] = scatter(C_RS + h, "col", c2_send.at[h], c2_recv.at[h])
+    out_pending = gather(O_AG, "row", o_all)
     for h in HALVES:
         arrived(flight[h])
         carried = total("col", c2_send.at[h], c2_recv.at[h])
         a_all[h, col] = (f_mine[:, pl.ds(128 * h, 128)] - carried).astype(BF16)
         flight[h] = gather(A_AG + h, "col", a_all.at[h])
-    arrived(out_pending)
-    o_recv[leaf] = o_all[...]
-    out_pending = start(O_X, "leaf", lambda there: o_all, lambda step: o_recv.at[leaf], o_recv.at[pl.ds(0, 3)])
 
     for h in HALVES:
         arrived(flight[h])
@@ -263,6 +261,9 @@
                 part = part + dot(child_t[x, a], a_all[h, pl.ds(4 * a, 4)].reshape(256, 128))
             d_send[h, pl.ds(4 * x, 4)] = part.reshape(4, 64, 128).astype(BF16)
         flight[h] = scatter(D_RS + h, "row", d_send.at[h], d_recv.at[h])
+    arrived(out_pending)
+    o_recv[leaf] = o_all[...]
+    out_pending = start(O_X, "leaf", lambda there: o_all, lambda step: o_recv.at[leaf], o_recv.at[pl.ds(0, 3)])
     for h in HALVES:
         arrived(flight[h])
         d_all[h, row] = total("row", d_send.at[h], d_recv.at[h]).astype(BF16)
@@ -273,15 +274,9 @@
             top, bottom = unpack(o_recv[2 * h, r], o_recv[2 * h + 1, r])
             root_out[:, pl.ds(32 * r, 16), pl.ds(128 * h, 128)] = top
             root_out[:, pl.ds(32 * r + 16, 16), pl.ds(128 * h, 128)] = bottom
-    root_store = pltpu.make_async_copy(root_out, root_out_h, local_sem.at[6])
-    root_store.start()
     for h in HALVES:
         arrived(flight[h])
         child_out[:, :, pl.ds(128 * h, 128)] = d_all[h]
-    child_store = pltpu.make_async_copy(child_out, child_out_h, local_sem.at[7])
-    child_store.start()
-    child_store.wait()
-    root_store.wait()
     for pending in sends:
         pending.wait_send()
 
@@ -296,7 +291,7 @@
     packed = (6, 16, 128)
     half = (2, 8, 64, 128)
     shapes = [
-        (2, 2, 256, 256), (2, 256, 256), (2, 3, 256, 256), (36, 256, 256), (6, 256, 256),
+        (2, 3, 256, 256), (36, 256, 256), (6, 256, 256),
         (2, 2, 256, 256), (3, 2, 256, 256), (36, 256, 256),
         (8, 64, 256), (8, 64, 256), None, (8, 64, 256),
         (4, 8, 3, 16, 128), (32, 3, 16, 128), None, (8,) + packed, (8,) + packed,
@@ -306,7 +301,7 @@
         (4, 3, 16, 128), (4, 8, 3, 16, 128), (3, 8, 2, 16, 128),
         half, half, half,
         half, half, half,
-        (8,) + packed, (4, 8) + packed, (8, 64, 256), (6, 256, 256),
+        (8,) + packed, (4, 8) + packed,
     ]
     wide = iter([(64, 256), (4, 3, 16, 128)])
     scratch = [
@@ -315,7 +310,7 @@
     scratch += [
         pltpu.VMEM((4, 1, 24), jnp.int32),
         pltpu.SMEM((4, 1, 24), jnp.int32),
-        pltpu.SemaphoreType.DMA((8,)),
+        pltpu.SemaphoreType.DMA((7,)),
         pltpu.SemaphoreType.DMA((TRANSFERS,)),
         pltpu.SemaphoreType.DMA((TRANSFERS,)),
     ]
@@ -325,11 +320,11 @@
             jax.ShapeDtypeStruct((8, 64, 256), BF16),
             jax.ShapeDtypeStruct((6, 256, 256), BF16),
         ),
-        in_specs=[away] * 5 + [near],
-        out_specs=(away, away),
+        in_specs=[near] * 2 + [away] * 4,
+        out_specs=(near, near),
         scratch_shapes=scratch,
         compiler_params=pltpu.CompilerParams(
-            collective_id=0, has_side_effects=True, vmem_limit_bytes=60 * 1024 * 1024
+            collective_id=0, has_side_effects=True, vmem_limit_bytes=207 * 256 * 1024
         ),
         cost_estimate=pl.CostEstimate(flops=3_000_000_000, bytes_accessed=10_000_000, transcendentals=0),
         name="substitution",

time: 107 us -> 105 us (0.981)
  Pallas kernels: 101 us -> 99.7 us
  other arithmetic: 3.29 us -> 2.11 us
    pallas_call x1, Pallas kernels: 101 us -> 99.7 us  [on_device(): pl.pallas_call(kernel, out_shape=(jax.ShapeDtypeStruct((8, 64, 256), BF16...]
    unnamed x2, other arithmetic: 3.29 us -> 2.11 us
    unnamed x3 -> x5, local copies, waits for them, and re-layouts: 1.91 us -> 2.71 us
where the time goes in v4:
time: 105 us
  Pallas kernels  99.7 us (95%)
  local copies, waits for them, and re-layouts  2.71 us (3%)
  other arithmetic  2.11 us (2%)
    pallas_call x1, Pallas kernels, on_device(): pl.pallas_call(kernel, out_shape=(jax.ShapeDtypeStruct((8, 64, 256), BF16...  99.7 us
    unnamed x5, local copies, waits for them, and re-layouts  2.71 us
    unnamed x2, other arithmetic  2.11 us

profile of v4, /device:TPU:1, one launch (start us, length us, event | category | flops | bytes accessed | tf_op | source)
XLA Modules:
  0.0 105.2 jit_solution(6998395324291855281)
XLA Ops:
  0.6 1.1 %copy.12 = bf16[1,2,1,256,2,1,256]{6,3,4,1,5,2,0:T(8,128)(2,1)S(1)} copy(bf16[1,2,1,256,2,1,256]{6,4,5,3,2,1,0:T(2,128)(2,1)} %param.7) | data formatting | bytes 1048576 | tf_op args[1]
  1.7 0.0 copy-start
  1.8 0.9 copy-done
  2.7 0.0 copy-start.1
  2.7 0.7 copy-done.1
  3.4 99.7 %substitution.1 = (bf16[8,64,256]{2,1,0:T(8,128)(2,1)S(1)}, bf16[6,256,256]{2,1,0:T(8,128)(2,1)S(1)}) custom-call(bf16[2,2,256,256]{3,2,1,0:T(8,128)(2,1)S(1)} %bitcast.26, bf16[2,256,256]{2,1,0:T(8,128)(2,1)S(1)} %bitcast.28, bf16[2,3,256,256]{3,2,1,0:T(8,128)(2,1)} %bitcast.30, bf16[36,256,256]{2,1,0:T(8,128)(2,1)} %bitcast.29, ...), custom_call_target="tpu_custom_call" | custom-call | flops 3000000000 | bytes 10000000 | tf_op jit(solution)/shard_map/substitution/pallas_call | solution.py:317
  103.1 1.3 %bitcast_convert_fusion = f32[6,1,256,256]{3,2,1,0:T(8,128)} fusion(bf16[6,256,256]{2,1,0:T(8,128)(2,1)S(1)} %get-tuple-element.5), kind=kLoop, calls=%fused_computation | loop fusion | flops 393216 | bytes 2359296
  104.3 0.8 convert.3
Async XLA Ops:
  1.7 1.0 copy-start
  2.7 0.7 copy-start.1

commit v5 on v4

--- a/solution.py
+++ b/solution.py
@@ -9,9 +9,9 @@
 BF16 = jnp.bfloat16
 MESH = pl.DeviceIdType.MESH
 
-N_XZ, C_RS, A_AG, D_RS, D_AG = range(0, 10, 2)
-F_RS, F_AG, L_XZ, L_C, U_AG, Y_RS, Y_AG, X_RS, X_C, S_X, O_AG, O_X = range(10, 22)
-TRANSFERS = 22
+N_XZ, C_CORE, C_Y, A_CORE, D_RS, D_AG = range(0, 12, 2)
+F_RS, F_AG, L_XZ, L_C, U_AG, Y_CORE, Y_Y, Y_BACK, X_RS, X_C, S_X, O_AG, O_X = range(12, 25)
+TRANSFERS = 25
 HALVES = (0, 1)
 FAR_FIRST = (4, 3, 5, 2, 6, 1, 7)
 
@@ -34,14 +34,16 @@
     child, rhs, link_h, root_h, root_rhs_h, structure_h,
     child_out, root_out,
     link, root, root_rhs, child_t, link_t, root_t,
-    f_send, f_recv, f_mine, f_all, l_send, l_recv, lx_all, c_send, c_recv,
-    u_all, spread, y_send, y_recv, y_all, x_send, x_recv, x_all, n_send, n_recv, n_all,
-    c2_send, c2_recv, a_all, d_send, d_recv, d_all, o_all, o_recv,
+    f_send, f_recv, f_all, l_send, l_recv, lx_all, c_send, c_recv,
+    u_all, spread, y_send, y_recv, y_pairs, y_all, x_send, x_recv, x_all, n_send, n_recv, n_all,
+    c2_send, c2_recv, c2_pairs, a_all, d_send, d_recv, d_all, o_all, o_recv,
     ids_v, ids, local_sem, send_sem, recv_sem,
 ):
     leaf, row, col = (lax.axis_index(a) for a in ("leaf", "row", "col"))
     place = {"leaf": leaf, "row": row, "col": col}
     size = {"leaf": 4, "row": 8, "col": 8}
+    core, chip = lax.rem(col, 2), col // 2
+    other = {"col": col + 1 - 2 * core}
     sends = []
 
     def peer(axis, step):
@@ -70,6 +72,23 @@
     def gather(number, axis, whole):
         mine = whole.at[place[axis]]
         return start(number, axis, lambda there: mine, lambda step: mine, whole.at[pl.ds(0, size[axis] - 1)])
+
+    def to_other_core(number, source, target):
+        pending = copy(number, number, source, target, other)
+        pending.start()
+        sends.append(pending)
+        return pending
+
+    def to_other_chips(number, whole):
+        mine = whole.at[chip]
+        for step in (2, 1, 3):
+            copy(number, number, mine, mine, {"col": 2 * lax.rem(chip + step, 4) + core}).start()
+        pending = copy(number, number, whole.at[pl.ds(0, 3)], whole.at[pl.ds(0, 3)], other)
+        sends.append(pending)
+        return pending
+
+    def over_chips(whole):
+        return (whole[0].astype(F32) + whole[1].astype(F32)) + (whole[2].astype(F32) + whole[3].astype(F32))
 
     def arrived(pending):
         pending.wait_recv()
@@ -116,8 +135,7 @@
         for m in range(3):
             link_t[m, a] = link[a, m].T
     arrived(pending)
-    f_mine[...] = total("col", f_send, f_recv)
-    f_all[col] = f_mine[...].astype(BF16)
+    f_all[col] = total("col", f_send, f_recv).astype(BF16)
     pending = gather(F_AG, "col", f_all)
     for a in range(2):
         for x in range(2):
@@ -132,13 +150,10 @@
             part = part.reshape(8, 2, 16, 128)
             for q, packed in enumerate(pack_quarters(part[:, 0], part[:, 1])):
                 l_send[2 * h + q, :, m] = packed.astype(BF16)
-        for step in FAR_FIRST:
-            for there in (2 * h, 2 * h + 1):
-                at = peer("row", step)
-                copy(L_XZ, L_XZ, l_send.at[there, at], l_recv.at[leaf * 8 + step], {"leaf": there, "row": at}).start()
-    for step in (2, 1, 3):
-        there = peer("leaf", step)
-        copy(L_XZ, L_XZ, l_send.at[there, row], l_recv.at[leaf * 8], {"leaf": there}).start()
+    for leaf_step in (2, 1, 3, 0):
+        for step in FAR_FIRST + ((0,) if leaf_step else ()):
+            there, at = peer("leaf", leaf_step), peer("row", step)
+            copy(L_XZ, L_XZ, l_send.at[there, at], l_recv.at[leaf * 8 + step], {"leaf": there, "row": at}).start()
     pltpu.make_async_copy(l_send.at[leaf, row], l_recv.at[leaf * 8], recv_sem.at[L_XZ]).start()
     pending = copy(L_XZ, L_XZ, l_recv.at[pl.ds(0, 31)], l_recv, {"row": peer("row", 1)})
     sends.append(pending)
@@ -195,15 +210,19 @@
                 value = value + dot(matrix[a * 6 + x], spread[x].reshape(256, 128))
             value = value + swap_halves(value)
             value = value.reshape(8, 2, 16, 128)
-            parts[:, a] = jnp.where(left, value[:, 0], value[:, 1]).astype(BF16)
+            parts[:, a] = jnp.where(left, value[:, 0], value[:, 1]).astype(parts.dtype)
 
     arrived(pending)
     spread_out(u_all)
     root_product(root, y_send)
-    pending = scatter(Y_RS, "col", y_send, y_recv)
-    arrived(pending)
-    y_all[col] = total("col", y_send, y_recv).astype(BF16)
-    pending = gather(Y_AG, "col", y_all)
+    mine, theirs = pl.ds(4 * core, 4), pl.ds(4 - 4 * core, 4)
+    pending = to_other_core(Y_CORE, y_send.at[theirs], y_recv)
+    arrived(pending)
+    y_pairs[chip] = (y_send[mine] + y_recv[...]).astype(BF16)
+    pending = to_other_chips(Y_Y, y_pairs)
+    arrived(pending)
+    y_all[mine] = over_chips(y_pairs).astype(BF16)
+    pending = to_other_core(Y_BACK, y_all.at[mine], y_all.at[mine])
     arrived(pending)
     spread_out(y_all)
     root_product(root_t, x_send)
@@ -220,8 +239,8 @@
             r = ids[child_at, 0, col + 8 * m]
             n_send[child_at, m] = x_all[r & 7, r >> 3]
     half_at = N_XZ + leaf // 2
-    for step in FAR_FIRST + (0,):
-        for leaf_step in (0, 1, 2, 3) if step else (1, 2, 3):
+    for leaf_step in (2, 1, 3, 0):
+        for step in FAR_FIRST + ((0,) if leaf_step else ()):
             there, at = peer("leaf", leaf_step), peer("row", step)
             copy(N_XZ, half_at, n_send.at[there], n_recv.at[leaf, row], {"leaf": there, "row": at}).start()
     pltpu.make_async_copy(n_send.at[leaf], n_recv.at[leaf, row], recv_sem.at[half_at]).start()
@@ -240,25 +259,30 @@
         arrived(copy(N_XZ, N_XZ + h, pieces, pieces, {"row": peer("row", 1)}))
         for m in range(3):
             n_all[m, :, 0], n_all[m, :, 1] = unpack(n_recv[2 * h, :, m], n_recv[2 * h + 1, :, m])
-        for a in range(2):
+        for n, a in enumerate((1 - core, core)):
             part = jnp.zeros((256, 128), F32)
             for m in range(3):
                 part = part + dot(link[a, m], n_all[m].reshape(256, 128))
-            c2_send[h, pl.ds(4 * a, 4)] = part.reshape(4, 64, 128).astype(BF16)
-        flight[h] = scatter(C_RS + h, "col", c2_send.at[h], c2_recv.at[h])
+            c2_send[h, n] = part
+            if n == 0:
+                flight[h] = to_other_core(C_CORE + h, c2_send.at[h, 0], c2_recv.at[h])
     out_pending = gather(O_AG, "row", o_all)
     for h in HALVES:
         arrived(flight[h])
-        carried = total("col", c2_send.at[h], c2_recv.at[h])
-        a_all[h, col] = (f_mine[:, pl.ds(128 * h, 128)] - carried).astype(BF16)
-        flight[h] = gather(A_AG + h, "col", a_all.at[h])
+        c2_pairs[h, chip] = (c2_send[h, 1] + c2_recv[h]).astype(BF16)
+        flight[h] = to_other_chips(C_Y + h, c2_pairs.at[h])
+    for h in HALVES:
+        arrived(flight[h])
+        known = f_all[pl.ds(4 * core, 4), :, pl.ds(128 * h, 128)].astype(F32)
+        a_all[h, core] = (known.reshape(256, 128) - over_chips(c2_pairs.at[h])).astype(BF16)
+        flight[h] = to_other_core(A_CORE + h, a_all.at[h, core], a_all.at[h, core])
 
     for h in HALVES:
         arrived(flight[h])
         for x in range(2):
             part = jnp.zeros((256, 128), F32)
             for a in range(2):
-                part = part + dot(child_t[x, a], a_all[h, pl.ds(4 * a, 4)].reshape(256, 128))
+                part = part + dot(child_t[x, a], a_all[h, a])
             d_send[h, pl.ds(4 * x, 4)] = part.reshape(4, 64, 128).astype(BF16)
         flight[h] = scatter(D_RS + h, "row", d_send.at[h], d_recv.at[h])
     arrived(out_pending)
@@ -293,20 +317,17 @@
     shapes = [
         (2, 3, 256, 256), (36, 256, 256), (6, 256, 256),
         (2, 2, 256, 256), (3, 2, 256, 256), (36, 256, 256),
-        (8, 64, 256), (8, 64, 256), None, (8, 64, 256),
-        (4, 8, 3, 16, 128), (32, 3, 16, 128), None, (8,) + packed, (8,) + packed,
+        (8, 64, 256), (8, 64, 256), (8, 64, 256),
+        (4, 8, 3, 16, 128), (32, 3, 16, 128), pltpu.VMEM((4, 3, 16, 128), F32), (8,) + packed, (8,) + packed,
         (8,) + packed, (6, 8, 2, 16, 128),
-        (8,) + packed, (8,) + packed, (8,) + packed,
+        pltpu.VMEM((8,) + packed, F32), pltpu.VMEM((4,) + packed, F32), (4, 4) + packed, (8,) + packed,
         (8,) + packed, (8,) + packed, (8,) + packed,
         (4, 3, 16, 128), (4, 8, 3, 16, 128), (3, 8, 2, 16, 128),
-        half, half, half,
+        pltpu.VMEM((2, 2, 256, 128), F32), pltpu.VMEM((2, 256, 128), F32), (2, 4, 256, 128), (2, 2, 256, 128),
         half, half, half,
         (8,) + packed, (4, 8) + packed,
     ]
-    wide = iter([(64, 256), (4, 3, 16, 128)])
-    scratch = [
-        pltpu.VMEM(next(wide), F32) if shape is None else pltpu.VMEM(shape, BF16) for shape in shapes
-    ]
+    scratch = [pltpu.VMEM(s, BF16) if isinstance(s, tuple) else s for s in shapes]
     scratch += [
         pltpu.VMEM((4, 1, 24), jnp.int32),
         pltpu.SMEM((4, 1, 24), jnp.int32),

time: 105 us -> 107 us (1.019)
  Pallas kernels: 99.7 us -> 101 us
    pallas_call x1, Pallas kernels: 99.7 us -> 101 us  [on_device(): pl.pallas_call(kernel, out_shape=(jax.ShapeDtypeStruct((8, 64, 256), BF16...]
where the time goes in v5:
time: 107 us
  Pallas kernels  101 us (94%)
  local copies, waits for them, and re-layouts  2.71 us (3%)
  other arithmetic  2.11 us (2%)
    pallas_call x1, Pallas kernels, on_device(): pl.pallas_call(kernel, out_shape=(jax.ShapeDtypeStruct((8, 64, 256), BF16...  101 us
    unnamed x5, local copies, waits for them, and re-layouts  2.71 us

profile of v5, /device:TPU:1, one launch (start us, length us, event | category | flops | bytes accessed | tf_op | source)
XLA Modules:
  0.0 106.7 jit_solution(1675881673553011111)
XLA Ops:
  0.6 1.1 %copy.12 = bf16[1,2,1,256,2,1,256]{6,3,4,1,5,2,0:T(8,128)(2,1)S(1)} copy(bf16[1,2,1,256,2,1,256]{6,4,5,3,2,1,0:T(2,128)(2,1)} %param.7) | data formatting | bytes 1048576 | tf_op args[1]
  1.7 0.0 copy-start
  1.8 0.9 copy-done
  2.7 0.0 copy-start.1
  2.7 0.7 copy-done.1
  3.4 101.3 %substitution.1 = (bf16[8,64,256]{2,1,0:T(8,128)(2,1)S(1)}, bf16[6,256,256]{2,1,0:T(8,128)(2,1)S(1)}) custom-call(bf16[2,2,256,256]{3,2,1,0:T(8,128)(2,1)S(1)} %bitcast.26, bf16[2,256,256]{2,1,0:T(8,128)(2,1)S(1)} %bitcast.28, bf16[2,3,256,256]{3,2,1,0:T(8,128)(2,1)} %bitcast.30, bf16[36,256,256]{2,1,0:T(8,128)(2,1)} %bitcast.29, ...), custom_call_target="tpu_custom_call" | custom-call | flops 3000000000 | bytes 10000000 | tf_op jit(solution)/shard_map/substitution/pallas_call | solution.py:338
  104.6 1.3 %bitcast_convert_fusion = f32[6,1,256,256]{3,2,1,0:T(8,128)} fusion(bf16[6,256,256]{2,1,0:T(8,128)(2,1)S(1)} %get-tuple-element.5), kind=kLoop, calls=%fused_computation | loop fusion | flops 393216 | bytes 2359296
  105.9 0.8 convert.3
Async XLA Ops:
  1.7 1.0 copy-start
  2.7 0.7 copy-start.1

commit v6 on v4

--- a/solution.py
+++ b/solution.py
@@ -31,12 +31,12 @@
 
 
 def kernel(
-    child, rhs, link_h, root_h, root_rhs_h, structure_h,
-    child_out, root_out,
-    link, root, root_rhs, child_t, link_t, root_t,
+    child_h, rhs_h, link_h, root_h, root_rhs_h, structure_h,
+    child_out_h, root_out_h,
+    raw, child, rhs, link, root, root_rhs, child_t, link_t, root_t,
     f_send, f_recv, f_mine, f_all, l_send, l_recv, lx_all, c_send, c_recv,
     u_all, spread, y_send, y_recv, y_all, x_send, x_recv, x_all, n_send, n_recv, n_all,
-    c2_send, c2_recv, a_all, d_send, d_recv, d_all, o_all, o_recv,
+    c2_send, c2_recv, a_all, d_send, d_recv, d_all, o_all, o_recv, root_out,
     ids_v, ids, local_sem, send_sem, recv_sem,
 ):
     leaf, row, col = (lax.axis_index(a) for a in ("leaf", "row", "col"))
@@ -87,11 +87,12 @@
         pltpu.make_async_copy(src, dst, local_sem.at[n])
         for n, (src, dst) in enumerate(
             (
-                (structure_h, ids_v.at[leaf]), (link_h, link), (root_rhs_h, root_rhs), (root_h, root),
+                (structure_h, ids_v.at[leaf]), (child_h, raw), (rhs_h, rhs), (link_h, link), (root_rhs_h, root_rhs), (root_h, root),
             )
         )
     ]
-    loads[0].start()
+    for n in (1, 2, 0):
+        loads[n].start()
     barrier = pltpu.get_barrier_semaphore()
     for step in range(1, 8):
         pl.semaphore_signal(barrier, inc=1, device_id={"col": peer("col", step)}, device_id_type=MESH)
@@ -99,19 +100,24 @@
         there = {"leaf": peer("leaf", step // 8), "row": peer("row", step % 8)}
         pl.semaphore_signal(barrier, inc=1, device_id=there, device_id_type=MESH)
 
+    loads[1].wait()
+    for a in range(2):
+        for x in range(2):
+            child[a, x] = raw[a, :, x, :]
+    loads[2].wait()
     for a in range(2):
         part = dot(child[a, 0], rhs[0]) + dot(child[a, 1], rhs[1])
         f_send[pl.ds(4 * a, 4)] = part.reshape(4, 64, 256).astype(BF16)
     pl.semaphore_wait(barrier, 38)
     pending = scatter(F_RS, "col", f_send, f_recv)
-    for load in loads[1:]:
+    for load in loads[3:]:
         load.start()
     loads[0].wait()
     mine = ids_v.at[leaf]
     structure_pending = start(
         S_X, "leaf", lambda there: structure_h, lambda step: ids_v.at[leaf], ids_v.at[pl.ds(0, 3)]
     )
-    loads[1].wait()
+    loads[3].wait()
     for a in range(2):
         for m in range(3):
             link_t[m, a] = link[a, m].T
@@ -132,18 +138,15 @@
             part = part.reshape(8, 2, 16, 128)
             for q, packed in enumerate(pack_quarters(part[:, 0], part[:, 1])):
                 l_send[2 * h + q, :, m] = packed.astype(BF16)
-        for step in FAR_FIRST:
-            for there in (2 * h, 2 * h + 1):
-                at = peer("row", step)
-                copy(L_XZ, L_XZ, l_send.at[there, at], l_recv.at[leaf * 8 + step], {"leaf": there, "row": at}).start()
-    for step in (2, 1, 3):
-        there = peer("leaf", step)
-        copy(L_XZ, L_XZ, l_send.at[there, row], l_recv.at[leaf * 8], {"leaf": there}).start()
+    for leaf_step in (2, 1, 3, 0):
+        for step in FAR_FIRST + ((0,) if leaf_step else ()):
+            there, at = peer("leaf", leaf_step), peer("row", step)
+            copy(L_XZ, L_XZ, l_send.at[there, at], l_recv.at[leaf * 8 + step], {"leaf": there, "row": at}).start()
     pltpu.make_async_copy(l_send.at[leaf, row], l_recv.at[leaf * 8], recv_sem.at[L_XZ]).start()
     pending = copy(L_XZ, L_XZ, l_recv.at[pl.ds(0, 31)], l_recv, {"row": peer("row", 1)})
     sends.append(pending)
-    loads[2].wait()
-    loads[3].wait()
+    loads[4].wait()
+    loads[5].wait()
 
     def turn(n, carry):
         a, x = n // 6, n % 6
@@ -152,7 +155,7 @@
 
     lax.fori_loop(0, 12, turn, 0)
     arrived(structure_pending)
-    to_scalars = pltpu.make_async_copy(ids_v, ids, local_sem.at[6])
+    to_scalars = pltpu.make_async_copy(ids_v, ids, local_sem.at[8])
     to_scalars.start()
     to_scalars.wait()
     arrived(pending)
@@ -274,24 +277,29 @@
             top, bottom = unpack(o_recv[2 * h, r], o_recv[2 * h + 1, r])
             root_out[:, pl.ds(32 * r, 16), pl.ds(128 * h, 128)] = top
             root_out[:, pl.ds(32 * r + 16, 16), pl.ds(128 * h, 128)] = bottom
+    stores = [pltpu.make_async_copy(root_out, root_out_h, local_sem.at[9])]
+    stores[0].start()
     for h in HALVES:
         arrived(flight[h])
-        child_out[:, :, pl.ds(128 * h, 128)] = d_all[h]
+        store = pltpu.make_async_copy(d_all.at[h], child_out_h.at[:, :, pl.ds(128 * h, 128)], local_sem.at[10 + h])
+        store.start()
+        stores.append(store)
+    for store in stores:
+        store.wait()
     for pending in sends:
         pending.wait_send()
 
 
 def on_device(child_rhs, child_inv, root_inv, coupling, root_rhs, structure):
-    child = child_inv[0, :, 0, :, :, 0, :].transpose(0, 2, 1, 3)
+    child = child_inv[0, :, 0, :, :, 0, :]
     rhs = child_rhs[0, :, 0]
     link = coupling[0, :, 0, :, :, 0, :].transpose(0, 2, 1, 3)
     root = root_inv[:, 0, :, :, 0, :].transpose(0, 2, 1, 3).reshape(36, 256, 256)
     away = pl.BlockSpec(memory_space=pltpu.HBM)
-    near = pl.BlockSpec(memory_space=pltpu.VMEM)
     packed = (6, 16, 128)
     half = (2, 8, 64, 128)
     shapes = [
-        (2, 3, 256, 256), (36, 256, 256), (6, 256, 256),
+        (2, 256, 2, 256), (2, 2, 256, 256), (2, 256, 256), (2, 3, 256, 256), (36, 256, 256), (6, 256, 256),
         (2, 2, 256, 256), (3, 2, 256, 256), (36, 256, 256),
         (8, 64, 256), (8, 64, 256), None, (8, 64, 256),
         (4, 8, 3, 16, 128), (32, 3, 16, 128), None, (8,) + packed, (8,) + packed,
@@ -301,7 +309,7 @@
         (4, 3, 16, 128), (4, 8, 3, 16, 128), (3, 8, 2, 16, 128),
         half, half, half,
         half, half, half,
-        (8,) + packed, (4, 8) + packed,
+        (8,) + packed, (4, 8) + packed, (6, 256, 256),
     ]
     wide = iter([(64, 256), (4, 3, 16, 128)])
     scratch = [
@@ -310,7 +318,7 @@
     scratch += [
         pltpu.VMEM((4, 1, 24), jnp.int32),
         pltpu.SMEM((4, 1, 24), jnp.int32),
-        pltpu.SemaphoreType.DMA((7,)),
+        pltpu.SemaphoreType.DMA((12,)),
         pltpu.SemaphoreType.DMA((TRANSFERS,)),
         pltpu.SemaphoreType.DMA((TRANSFERS,)),
     ]
@@ -320,11 +328,11 @@
             jax.ShapeDtypeStruct((8, 64, 256), BF16),
             jax.ShapeDtypeStruct((6, 256, 256), BF16),
         ),
-        in_specs=[near] * 2 + [away] * 4,
-        out_specs=(near, near),
+        in_specs=[away] * 6,
+        out_specs=(away, away),
         scratch_shapes=scratch,
         compiler_params=pltpu.CompilerParams(
-            collective_id=0, has_side_effects=True, vmem_limit_bytes=207 * 256 * 1024
+            collective_id=0, has_side_effects=True, vmem_limit_bytes=60 * 1024 * 1024
         ),
         cost_estimate=pl.CostEstimate(flops=3_000_000_000, bytes_accessed=10_000_000, transcendentals=0),
         name="substitution",

time: 105 us -> 105 us (level)
  local copies, waits for them, and re-layouts: 2.71 us -> 0.01 us
  Pallas kernels: 99.7 us -> 101 us
  other arithmetic: 2.11 us -> 3.29 us
    unnamed x5 -> x2, local copies, waits for them, and re-layouts: 2.71 us -> 0.01 us
    pallas_call x1, Pallas kernels: 99.7 us -> 101 us  [on_device(): pl.pallas_call(kernel, out_shape=(jax.ShapeDtypeStruct((8, 64, 256), BF16...]
    unnamed x2, other arithmetic: 2.11 us -> 3.29 us
where the time goes in v6:
time: 105 us
  Pallas kernels  101 us (96%)
  other arithmetic  3.29 us (3%)
    pallas_call x1, Pallas kernels, on_device(): pl.pallas_call(kernel, out_shape=(jax.ShapeDtypeStruct((8, 64, 256), BF16...  101 us
    unnamed x2, other arithmetic  3.29 us

profile of v6, /device:TPU:1, one launch (start us, length us, event | category | flops | bytes accessed | tf_op | source)
XLA Modules:
  0.0 105.1 jit_solution(798779034258064578)
XLA Ops:
  0.6 101.2 %substitution.1 = (bf16[8,64,256]{2,1,0:T(8,128)(2,1)}, bf16[6,256,256]{2,1,0:T(8,128)(2,1)}) custom-call(bf16[2,256,2,256]{3,2,1,0:T(2,128)(2,1)} %bitcast.26, bf16[2,256,256]{2,1,0:T(8,128)(2,1)} %bitcast.27, bf16[2,3,256,256]{3,2,1,0:T(8,128)(2,1)} %bitcast.24, bf16[36,256,256]{2,1,0:T(8,128)(2,1)} %bitcast.23, bf16[6,256,256]{2,1,0:T(8,128)(2,1)} %bitcast.25, ...), custom_call_target="tpu_custom_call" | custom-call | flops 3000000000 | bytes 10000000 | tf_op jit(solution)/shard_map/substitution/pallas_call | solution.py:325
  101.8 0.0 copy-start
  101.8 2.5 %bitcast_convert_fusion = f32[6,1,256,256]{3,2,1,0:T(8,128)} fusion(bf16[6,256,256]{2,1,0:T(8,128)(2,1)} %get-tuple-element.5), kind=kLoop, calls=%fused_computation | loop fusion | flops 393216 | bytes 2359296
  104.3 0.0 copy-done
  104.3 0.8 convert.3
Async XLA Ops:
  101.8 2.5 %copy-start = (bf16[8,64,256]{2,1,0:T(8,128)(2,1)S(1)}, bf16[8,64,256]{2,1,0:T(8,128)(2,1)}, u32[]{:S(2)}) copy-start(bf16[8,64,256]{2,1,0:T(8,128)(2,1)} %get-tuple-element.4) | copy-start | bytes 786436

commit v7 on v6

--- a/solution.py
+++ b/solution.py
@@ -130,18 +130,20 @@
             child_t[x, a] = child[a, x].T
     arrived(pending)
 
-    for h in HALVES:
+    near, side = leaf // 2, lax.rem(leaf, 2)
+    for h in (1 - near, near):
+        lanes = pl.ds(pl.multiple_of(128 * h, 128), 128)
         for m in range(3):
             part = jnp.zeros((256, 128), F32)
             for a in range(2):
-                part = part + dot(link_t[m, a], f_all[pl.ds(4 * a, 4), :, pl.ds(128 * h, 128)].reshape(256, 128))
+                part = part + dot(link_t[m, a], f_all[pl.ds(4 * a, 4), :, lanes].reshape(256, 128))
             part = part.reshape(8, 2, 16, 128)
             for q, packed in enumerate(pack_quarters(part[:, 0], part[:, 1])):
                 l_send[2 * h + q, :, m] = packed.astype(BF16)
-    for leaf_step in (2, 1, 3, 0):
-        for step in FAR_FIRST + ((0,) if leaf_step else ()):
-            there, at = peer("leaf", leaf_step), peer("row", step)
-            copy(L_XZ, L_XZ, l_send.at[there, at], l_recv.at[leaf * 8 + step], {"leaf": there, "row": at}).start()
+        for n, there in enumerate((2 * h + side, 2 * h + 1 - side) if h is not near else (2 * h + 1 - side, leaf)):
+            for step in FAR_FIRST + (() if h is near and n else (0,)):
+                at = peer("row", step)
+                copy(L_XZ, L_XZ, l_send.at[there, at], l_recv.at[leaf * 8 + step], {"leaf": there, "row": at}).start()
     pltpu.make_async_copy(l_send.at[leaf, row], l_recv.at[leaf * 8], recv_sem.at[L_XZ]).start()
     pending = copy(L_XZ, L_XZ, l_recv.at[pl.ds(0, 31)], l_recv, {"row": peer("row", 1)})
     sends.append(pending)
@@ -216,6 +218,7 @@
     x_all[col] = solved
     pending = gather(X_C, "col", x_all)
     o_all[row] = solved
+    out_pending = gather(O_AG, "row", o_all)
     arrived(pending)
 
     for child_at in range(4):
@@ -249,7 +252,9 @@
                 part = part + dot(link[a, m], n_all[m].reshape(256, 128))
             c2_send[h, pl.ds(4 * a, 4)] = part.reshape(4, 64, 128).astype(BF16)
         flight[h] = scatter(C_RS + h, "col", c2_send.at[h], c2_recv.at[h])
-    out_pending = gather(O_AG, "row", o_all)
+    arrived(out_pending)
+    o_recv[leaf] = o_all[...]
+    out_pending = start(O_X, "leaf", lambda there: o_all, lambda step: o_recv.at[leaf], o_recv.at[pl.ds(0, 3)])
     for h in HALVES:
         arrived(flight[h])
         carried = total("col", c2_send.at[h], c2_recv.at[h])
@@ -264,9 +269,6 @@
                 part = part + dot(child_t[x, a], a_all[h, pl.ds(4 * a, 4)].reshape(256, 128))
             d_send[h, pl.ds(4 * x, 4)] = part.reshape(4, 64, 128).astype(BF16)
         flight[h] = scatter(D_RS + h, "row", d_send.at[h], d_recv.at[h])
-    arrived(out_pending)
-    o_recv[leaf] = o_all[...]
-    out_pending = start(O_X, "leaf", lambda there: o_all, lambda step: o_recv.at[leaf], o_recv.at[pl.ds(0, 3)])
     for h in HALVES:
         arrived(flight[h])
         d_all[h, row] = total("row", d_send.at[h], d_recv.at[h]).astype(BF16)

time: 105 us -> 105 us (level)
  no operation moved by 1% of the time
where the time goes in v7:
time: 105 us
  Pallas kernels  101 us (96%)
  other arithmetic  3.29 us (3%)
    pallas_call x1, Pallas kernels, on_device(): pl.pallas_call(kernel, out_shape=(jax.ShapeDtypeStruct((8, 64, 256), BF16...  101 us
    unnamed x2, other arithmetic  3.29 us

profile of v7, /device:TPU:1, one launch (start us, length us, event | category | flops | bytes accessed | tf_op | source)
XLA Modules:
  0.0 104.7 jit_solution(14666572856252308473)
XLA Ops:
  0.6 100.8 %substitution.1 = (bf16[8,64,256]{2,1,0:T(8,128)(2,1)}, bf16[6,256,256]{2,1,0:T(8,128)(2,1)}) custom-call(bf16[2,256,2,256]{3,2,1,0:T(2,128)(2,1)} %bitcast.26, bf16[2,256,256]{2,1,0:T(8,128)(2,1)} %bitcast.27, bf16[2,3,256,256]{3,2,1,0:T(8,128)(2,1)} %bitcast.24, bf16[36,256,256]{2,1,0:T(8,128)(2,1)} %bitcast.23, bf16[6,256,256]{2,1,0:T(8,128)(2,1)} %bitcast.25, ...), custom_call_target="tpu_custom_call" | custom-call | flops 3000000000 | bytes 10000000 | tf_op jit(solution)/shard_map/substitution/pallas_call | solution.py:327
  101.4 0.0 copy-start
  101.4 2.5 %bitcast_convert_fusion = f32[6,1,256,256]{3,2,1,0:T(8,128)} fusion(bf16[6,256,256]{2,1,0:T(8,128)(2,1)} %get-tuple-element.5), kind=kLoop, calls=%fused_computation | loop fusion | flops 393216 | bytes 2359296
  103.9 0.0 copy-done
  103.9 0.8 convert.3
Async XLA Ops:
  101.4 2.5 %copy-start = (bf16[8,64,256]{2,1,0:T(8,128)(2,1)S(1)}, bf16[8,64,256]{2,1,0:T(8,128)(2,1)}, u32[]{:S(2)}) copy-start(bf16[8,64,256]{2,1,0:T(8,128)(2,1)} %get-tuple-element.4) | copy-start | bytes 786436

commit v8 on v6

--- a/solution.py
+++ b/solution.py
@@ -138,10 +138,13 @@
             part = part.reshape(8, 2, 16, 128)
             for q, packed in enumerate(pack_quarters(part[:, 0], part[:, 1])):
                 l_send[2 * h + q, :, m] = packed.astype(BF16)
-    for leaf_step in (2, 1, 3, 0):
-        for step in FAR_FIRST + ((0,) if leaf_step else ()):
-            there, at = peer("leaf", leaf_step), peer("row", step)
-            copy(L_XZ, L_XZ, l_send.at[there, at], l_recv.at[leaf * 8 + step], {"leaf": there, "row": at}).start()
+        for step in FAR_FIRST:
+            for there in (2 * h, 2 * h + 1):
+                at = peer("row", step)
+                copy(L_XZ, L_XZ, l_send.at[there, at], l_recv.at[leaf * 8 + step], {"leaf": there, "row": at}).start()
+    for step in (2, 1, 3):
+        there = peer("leaf", step)
+        copy(L_XZ, L_XZ, l_send.at[there, row], l_recv.at[leaf * 8], {"leaf": there}).start()
     pltpu.make_async_copy(l_send.at[leaf, row], l_recv.at[leaf * 8], recv_sem.at[L_XZ]).start()
     pending = copy(L_XZ, L_XZ, l_recv.at[pl.ds(0, 31)], l_recv, {"row": peer("row", 1)})
     sends.append(pending)

time: 105 us -> 104 us (level)
    pallas_call x1, Pallas kernels: 101 us -> 100 us  [on_device(): pl.pallas_call(kernel, out_shape=(jax.ShapeDtypeStruct((8, 64, 256), BF16...]
where the time goes in v8:
time: 104 us
  Pallas kernels  100 us (96%)
  other arithmetic  3.29 us (3%)
    pallas_call x1, Pallas kernels, on_device(): pl.pallas_call(kernel, out_shape=(jax.ShapeDtypeStruct((8, 64, 256), BF16...  100 us
    unnamed x2, other arithmetic  3.29 us

profile of v8, /device:TPU:1, one launch (start us, length us, event | category | flops | bytes accessed | tf_op | source)
XLA Modules:
  0.0 104.1 jit_solution(3360555899785594262)
XLA Ops:
  0.6 100.1 %substitution.1 = (bf16[8,64,256]{2,1,0:T(8,128)(2,1)}, bf16[6,256,256]{2,1,0:T(8,128)(2,1)}) custom-call(bf16[2,256,2,256]{3,2,1,0:T(2,128)(2,1)} %bitcast.26, bf16[2,256,256]{2,1,0:T(8,128)(2,1)} %bitcast.27, bf16[2,3,256,256]{3,2,1,0:T(8,128)(2,1)} %bitcast.24, bf16[36,256,256]{2,1,0:T(8,128)(2,1)} %bitcast.23, bf16[6,256,256]{2,1,0:T(8,128)(2,1)} %bitcast.25, ...), custom_call_target="tpu_custom_call" | custom-call | flops 3000000000 | bytes 10000000 | tf_op jit(solution)/shard_map/substitution/pallas_call | solution.py:328
  100.8 0.0 copy-start
  100.8 2.5 %bitcast_convert_fusion = f32[6,1,256,256]{3,2,1,0:T(8,128)} fusion(bf16[6,256,256]{2,1,0:T(8,128)(2,1)} %get-tuple-element.5), kind=kLoop, calls=%fused_computation | loop fusion | flops 393216 | bytes 2359296
  103.2 0.0 copy-done
  103.2 0.8 convert.3
Async XLA Ops:
  100.8 2.5 %copy-start = (bf16[8,64,256]{2,1,0:T(8,128)(2,1)S(1)}, bf16[8,64,256]{2,1,0:T(8,128)(2,1)}, u32[]{:S(2)}) copy-start(bf16[8,64,256]{2,1,0:T(8,128)(2,1)} %get-tuple-element.4) | copy-start | bytes 786436

commit v9 on v8

--- a/solution.py
+++ b/solution.py
@@ -10,8 +10,8 @@
 MESH = pl.DeviceIdType.MESH
 
 N_XZ, C_RS, A_AG, D_RS, D_AG = range(0, 10, 2)
-F_RS, F_AG, L_XZ, L_C, U_AG, Y_RS, Y_AG, X_RS, X_C, S_X, O_AG, O_X = range(10, 22)
-TRANSFERS = 22
+F_RS, F_AG, L_XZ, L_C, U_AG, Y_RS, Y_AG, X_RS, X_C, S_X, O_AG, O_X, X_RS2 = range(10, 23)
+TRANSFERS = 23
 HALVES = (0, 1)
 FAR_FIRST = (4, 3, 5, 2, 6, 1, 7)
 
@@ -194,8 +194,8 @@
             spread[a, :, 0] = whole[:, a] * keep_left
             spread[a, :, 1] = whole[:, a] * keep_right
 
-    def root_product(matrix, parts):
-        for a in range(6):
+    def root_product(matrix, parts, rows=range(6)):
+        for a in rows:
             value = jnp.zeros((256, 128), F32)
             for x in range(6):
                 value = value + dot(matrix[a * 6 + x], spread[x].reshape(256, 128))
@@ -212,9 +212,16 @@
     pending = gather(Y_AG, "col", y_all)
     arrived(pending)
     spread_out(y_all)
-    root_product(root_t, x_send)
-    pending = scatter(X_RS, "row", x_send, x_recv)
-    arrived(pending)
+    parts = []
+    for number, first in ((X_RS, 0), (X_RS2, 3)):
+        root_product(root_t, x_send, range(first, first + 3))
+        rows = pl.ds(first, 3)
+        parts.append(start(
+            number, "row", lambda there: x_send.at[there, rows], lambda step: x_recv.at[step, rows],
+            x_send.at[pl.ds(0, 7), rows],
+        ))
+    for pending in parts:
+        arrived(pending)
     solved = total("row", x_send, x_recv).astype(BF16)
     x_all[col] = solved
     pending = gather(X_C, "col", x_all)

time: 104 us -> 104 us (level)
  no operation moved by 1% of the time
where the time goes in v9:
time: 104 us
  Pallas kernels  99.6 us (96%)
  other arithmetic  3.29 us (3%)
    pallas_call x1, Pallas kernels, on_device(): pl.pallas_call(kernel, out_shape=(jax.ShapeDtypeStruct((8, 64, 256), BF16...  99.6 us
    unnamed x2, other arithmetic  3.29 us

profile of v9, /device:TPU:1, one launch (start us, length us, event | category | flops | bytes accessed | tf_op | source)
XLA Modules:
  0.0 103.6 jit_solution(1456818335607875044)
XLA Ops:
  0.6 99.6 %substitution.1 = (bf16[8,64,256]{2,1,0:T(8,128)(2,1)}, bf16[6,256,256]{2,1,0:T(8,128)(2,1)}) custom-call(bf16[2,256,2,256]{3,2,1,0:T(2,128)(2,1)} %bitcast.26, bf16[2,256,256]{2,1,0:T(8,128)(2,1)} %bitcast.27, bf16[2,3,256,256]{3,2,1,0:T(8,128)(2,1)} %bitcast.24, bf16[36,256,256]{2,1,0:T(8,128)(2,1)} %bitcast.23, bf16[6,256,256]{2,1,0:T(8,128)(2,1)} %bitcast.25, ...), custom_call_target="tpu_custom_call" | custom-call | flops 3000000000 | bytes 10000000 | tf_op jit(solution)/shard_map/substitution/pallas_call | solution.py:335
  100.3 0.0 copy-start
  100.3 2.5 %bitcast_convert_fusion = f32[6,1,256,256]{3,2,1,0:T(8,128)} fusion(bf16[6,256,256]{2,1,0:T(8,128)(2,1)} %get-tuple-element.5), kind=kLoop, calls=%fused_computation | loop fusion | flops 393216 | bytes 2359296
  102.8 0.0 copy-done
  102.8 0.8 convert.3
Async XLA Ops:
  100.3 2.5 %copy-start = (bf16[8,64,256]{2,1,0:T(8,128)(2,1)S(1)}, bf16[8,64,256]{2,1,0:T(8,128)(2,1)}, u32[]{:S(2)}) copy-start(bf16[8,64,256]{2,1,0:T(8,128)(2,1)} %get-tuple-element.4) | copy-start | bytes 786436
